TPU v7x, 512 devices: a whole 4x4x16 slice. The times are simulated.
512 devices in a mesh: tm: 32 (over x, y, core), space: 16 (over z).
Axes of the slice: x: 4, y: 4, z: 16, core: 2. Of those that a mesh axis runs over, the one named last changes fastest.
Arguments:
- video_tokens: bfloat16 [32, 64, 64, 1152], P('tm', 'space'), may hold values from -6 to 6
- qkv_weight: bfloat16 [1152, 3456], P('space'), may hold values from -0.1875 to 0.1875
- out_weight: bfloat16 [1152, 1152], P('space'), may hold values from -0.1875 to 0.1875
- conv_weight: float32 [3, 3, 1152], replicated, may hold values from -2 to 2
- norm_gain: float32 [1152], replicated, may hold values from 0.1 to 1.9
Outputs:
- attended: bfloat16 [32, 64, 64, 1152], P('tm', 'space')
All inputs are finite; a program needn't handle non-finite values.
Results may differ from a plain program's by a relative error of at most 0.015.
Values may be sent and summed in bfloat16 or wider, within the bound.
A program may use at most 64 MiB of HBM per device.

v0:
```python
import jax
import jax.numpy as jnp
from jax import lax
from jax.sharding import PartitionSpec as P

HEADS = 36
HEAD_DIM = 32


def entering(value, axis, combine, identity):
    devices, place = (lax.axis_size(axis), lax.axis_index(axis))
    everything = lax.all_gather(value.astype(jnp.bfloat16), axis)
    start = jnp.broadcast_to(jnp.asarray(identity, value.dtype), value.shape)

    def lap(k, before):
        reached = k < place
        new = combine(before, everything[k].astype(value.dtype))
        return jnp.where(reached, new, before)

    return lax.fori_loop(0, devices, lap, start)


def with_halo(block, sides, width):
    for axis, dim in sides:
        count = lax.axis_size(axis)
        forward = [(i, i + 1) for i in range(count - 1)]
        backward = [(target, source) for source, target in forward]
        low = lax.ppermute(
            lax.slice_in_dim(block, block.shape[dim] - width, None, axis=dim), axis, forward
        )
        high = lax.ppermute(lax.slice_in_dim(block, 0, width, axis=dim), axis, backward)
        block = jnp.concatenate([low, block, high], axis=dim)
    return block


def fold_product(left_side, block_rows):
    return jnp.dot(left_side, block_rows, preferred_element_type=jnp.float32)


def add_states(earlier, later):
    return earlier + later


def causal_states(key_feat, values):
    key_heads = key_feat.reshape(-1, HEADS, HEAD_DIM)
    value_heads = values.reshape(-1, HEADS, HEAD_DIM)
    frame_state = jnp.einsum(
        "thd,the->hde", key_heads, value_heads, preferred_element_type=jnp.float32
    )
    flat_state = frame_state.reshape(-1)
    frame_sum = lax.psum(flat_state.astype(jnp.bfloat16), "space").astype(jnp.float32)
    earlier = entering(frame_sum, "tm", add_states, jnp.zeros_like(frame_sum))
    whole_state = earlier + frame_sum
    return whole_state.reshape(HEADS, HEAD_DIM, HEAD_DIM)


def per_device(video_tokens, qkv_weight, out_weight, conv_weight, norm_gain):
    frame_now = video_tokens[0]
    row_count, col_count, feat_width = frame_now.shape
    tokens = frame_now.reshape(row_count * col_count, feat_width)
    projected = fold_product(tokens, lax.all_gather(qkv_weight, "space", axis=0, tiled=True))
    query_feat = jax.nn.relu(projected[:, :feat_width]).astype(jnp.bfloat16)
    key_feat = jax.nn.relu(projected[:, feat_width : 2 * feat_width]).astype(jnp.bfloat16)
    values = projected[:, 2 * feat_width :].astype(jnp.bfloat16)
    state_all = causal_states(key_feat, values)
    padded_rows = with_halo(values.reshape(row_count, col_count, feat_width), (("space", 0),), 1)
    padded = jnp.pad(padded_rows, ((0, 0), (1, 1), (0, 0))).astype(jnp.float32)
    local_term = jnp.zeros((row_count, col_count, feat_width), jnp.float32)
    for row_shift in range(3):
        for col_shift in range(3):
            local_term = (
                local_term
                + conv_weight[row_shift, col_shift]
                * padded[row_shift : row_shift + row_count, col_shift : col_shift + col_count]
            )
    state_low = state_all.astype(jnp.bfloat16)
    query_heads = query_feat.reshape(-1, HEADS, HEAD_DIM)
    readout = jnp.einsum("thd,hde->the", query_heads, state_low, preferred_element_type=jnp.float32)
    readout = readout.reshape(-1, feat_width)
    mean_square = jnp.mean(readout * readout, axis=-1, keepdims=True)
    normed = readout * lax.rsqrt(mean_square + 1e-06) * norm_gain
    mixture = (normed + local_term.reshape(-1, feat_width)).astype(jnp.bfloat16)
    result = fold_product(mixture, lax.all_gather(out_weight, "space", axis=0, tiled=True))
    return result.astype(jnp.bfloat16).reshape(1, row_count, col_count, feat_width)


def solution(mesh):
    in_specs = (P("tm", "space", None, None), P("space", None), P("space", None), P(), P())
    out_specs = P("tm", "space", None, None)
    return jax.shard_map(
        per_device, mesh=mesh, in_specs=in_specs, out_specs=out_specs, check_vma=False
    )
```

profile of v0, /device:TPU:30, one launch (start us, length us, event | category | flops | bytes accessed | tf_op | source)
XLA Modules:
  0.0 405.9 jit_solution(9522417113810979883)
XLA Ops:
  7.3 108.0 %all-gather.5.cloned.1.call-done = bf16[1152,3456]{1,0:T(8,128)(2,1)} async-done(((bf16[72,3456]{1,0:T(8,128)(2,1)}), bf16[1152,3456]{1,0:T(8,128)(2,1)}) %all-gather.5.cloned.1.call-update) | async-done | bytes 7962640 | tf_op jit(solution)/shard_map/all_gather | solution.py:61
  115.3 5.8 %fusion.21 = bf16[256,3456]{1,0:T(8,128)(2,1)S(1)} fusion(bf16[256,1152]{1,0:T(8,128)(2,1)S(1)} %bitcast.35, bf16[1152,3456]{1,0:T(8,128)(2,1)} %all-gather.5.cloned.1.call-done), kind=kOutput, calls=%fused_computation.53 | convolution fusion | flops 2038431744 | bytes 10321920 | tf_op jit(solution)/shard_map/dot_general | solution.py:37
  121.1 1.2 fusion.9
  123.4 2.1 copy.15
  125.5 1.5 convolution_convert_fusion.1
  127.9 131.5 %all-reduce.3.cloned.1.call-done = bf16[36864]{0:T(1024)(128)(2,1)} async-done(((bf16[36864]{0:T(1024)(128)(2,1)}), bf16[36864]{0:T(1024)(128)(2,1)}) %all-reduce.3.cloned.1.call-update) | async-done | bytes 73744 | tf_op jit(solution)/shard_map/psum | solution.py:51
  259.5 3.5 collective-permute-start
  263.0 1.3 collective-permute-start.1
  265.4 2.1 copy.17
  267.5 2.6 collective-permute-done.1
  271.5 44.8 %all-gather.9.cloned.1.call-done = bf16[1179648]{0:T(1024)(128)(2,1)} async-done(((bf16[36864]{0:T(1024)(128)(2,1)}), bf16[1179648]{0:T(1024)(128)(2,1)}) %all-gather.9.cloned.1.call-update) | async-done | bytes 2359312 | tf_op jit(solution)/shard_map/all_gather | solution.py:12
  316.4 4.3 %reshape.46 = bf16[32,36864]{1,0:T(8,128)(2,1)} reshape(bf16[1179648]{0:T(1024)(128)(2,1)} %all-gather.9.cloned.1.call-done) | data formatting | bytes 4718592 | tf_op jit(solution)/shard_map/all_gather | solution.py:12
  320.7 40.4 %while.14 = (s32[]{:T(128)}, f32[36864]{0:T(1024)S(1)}, s32[]{:T(128)}, bf16[32,36864]{1,0:T(8,128)(2,1)}, s32[]{:T(128)}, /*index=5*/s32[]{:T(128)}) while((s32[]{:T(128)}, f32[36864]{0:T(1024)S(1)}, s32[]{:T(128)}, bf16[32,36864]{1,0:T(8,128)(2,1)}, s32[]{:T(128)}, /*index=5*/s32[]{:T(128)}) %tuple.44), condition=%wide.region_2.3_spmd.clone, body=%wide.region_1.2_spmd.clone.sunk | while | flops 147460 | bytes 663645 | solution.py:20
  320.7 1.2 dynamic-slice_convert_fusion.2
  322.0 1.2 dynamic-slice_convert_fusion.2
  323.3 1.2 dynamic-slice_convert_fusion.2
  324.5 1.2 dynamic-slice_convert_fusion.2
  325.8 1.2 dynamic-slice_convert_fusion.2
  327.0 1.2 dynamic-slice_convert_fusion.2
  328.3 1.2 dynamic-slice_convert_fusion.2
  329.6 1.2 dynamic-slice_convert_fusion.2
  332.1 1.2 dynamic-slice_convert_fusion.2
  333.3 1.2 dynamic-slice_convert_fusion.2
  334.6 1.2 dynamic-slice_convert_fusion.2
  335.8 1.2 dynamic-slice_convert_fusion.2
  342.2 1.2 dynamic-slice_convert_fusion.2
  346.0 1.2 dynamic-slice_convert_fusion.2
  349.7 1.2 dynamic-slice_convert_fusion.2
  353.5 1.2 dynamic-slice_convert_fusion.2
  358.6 1.2 dynamic-slice_convert_fusion.2
  362.1 33.7 %all-gather.7.cloned.1.call-done = bf16[1152,1152]{1,0:T(8,128)(2,1)} async-done(((bf16[72,1152]{1,0:T(8,128)(2,1)}), bf16[1152,1152]{1,0:T(8,128)(2,1)}) %all-gather.7.cloned.1.call-update) | async-done | bytes 2654224 | tf_op jit(solution)/shard_map/all_gather | solution.py:83
  395.8 3.6 convolution_convert_fusion
  (77 shorter events, 25.5 us)
Async XLA Ops:
  6.5 108.7 %copy-start = (bf16[1,4,64,1152]{3,2,1,0:T(8,128)(2,1)S(1)}, bf16[1,4,64,1152]{3,2,1,0:T(8,128)(2,1)}, u32[]{:S(2)}) copy-start(bf16[1,4,64,1152]{3,2,1,0:T(8,128)(2,1)} %param.7) | copy-start | bytes 1769476
  6.5 108.7 %all-gather.5.cloned.1.call-start = ((), (), s32[]{:S(2)}) async-start(), calls=%async_computation | async-start | bytes 8460288 | tf_op jit(solution)/shard_map/all_gather | solution.py:61
  7.3 252.2 %all-reduce.3.cloned.1.call-start = ((), (), s32[]{:S(2)}) async-start(), calls=%async_computation.1 | async-start | bytes 147456 | tf_op jit(solution)/shard_map/psum | solution.py:51
  127.9 188.5 %all-gather.9.cloned.1.call-start = ((), (), s32[]{:S(2)}) async-start(), calls=%async_computation.3 | async-start | bytes 2433024 | tf_op jit(solution)/shard_map/all_gather | solution.py:12
  259.4 136.3 %all-gather.7.cloned.1.call-start = ((), (), s32[]{:S(2)}) async-start(), calls=%async_computation.2 | async-start | bytes 2820096 | tf_op jit(solution)/shard_map/all_gather | solution.py:83
  259.5 7.9 %collective-permute-start = (bf16[1,64,1152]{2,1,0:T(8,128)(2,1)S(1)}, bf16[1,64,1152]{2,1,0:T(8,128)(2,1)S(1)}, u32[]{:S(2)}, u32[]{:S(2)}) collective-permute-start(bf16[1,64,1152]{2,1,0:T(8,128)(2,1)S(1)} %get-tuple-element.120), channel_id=1, source_target_pairs={{0,1},{1,2},{2,3},{3,4},{4,5},{5,6},{6,7},{7,8},{8,9},{9,10},{10,1... | collective-permute-start | bytes 442376 | tf_op jit(solution)/shard_map/ppermute | solution.py:28
  263.0 7.0 %collective-permute-start.1 = (bf16[1,64,1152]{2,1,0:T(8,128)(2,1)S(1)}, bf16[1,64,1152]{2,1,0:T(8,128)(2,1)S(1)}, u32[]{:S(2)}, u32[]{:S(2)}) collective-permute-start(bf16[1,64,1152]{2,1,0:T(8,128)(2,1)S(1)} %get-tuple-element.121), channel_id=1, source_target_pairs={{1,0},{2,1},{3,2},{4,3},{5,4},{6,5},{7,6},{8,7},{9,8},{10,9},{11,1... | collective-permute-start | bytes 442376 | tf_op jit(solution)/shard_map/ppermute | solution.py:31
  320.7 40.4 %copy-start.2 = (bf16[36864]{0:T(1024)(128)(2,1)S(1)}, bf16[36864]{0:T(1024)(128)(2,1)}, u32[]{:S(2)}) copy-start(bf16[36864]{0:T(1024)(128)(2,1)} %all-reduce.3.cloned.1.call-done) | copy-start | bytes 221188
  320.7 40.6 %copy-start.1 = (bf16[256,1152]{0,1:T(8,128)(2,1)S(1)}, bf16[256,1152]{0,1:T(8,128)(2,1)}, u32[]{:S(2)}) copy-start(bf16[256,1152]{0,1:T(8,128)(2,1)} %copy.17) | copy-start | bytes 1769476
  361.1 0.7 copy-start.3
Sparse Core Ops, SparseCore 0:
  9.4 105.7 all-gather.4
  128.0 131.3 all-reduce.2
  263.0 53.2 all-gather.8
  318.5 77.2 all-gather.6
where the time goes:
time: 408 us; the launch traced here: 406 us
  waiting for transfers between devices  321 us (79%)
  other arithmetic  42.1 us (10%)
  between operations  13.3 us (3%)
  local copies, waits for them, and re-layouts  12.1 us (3%)
  matrix products  11.3 us (3%)
  starting transfers between devices  4.89 us (1%)
    psum x1, waiting for transfers between devices, causal_states(): lax.psum(flat_state.astype(jnp.bfloat16), 'space').astype(jnp.float32)  132 us
    all_gather x1, waiting for transfers between devices, per_device(): lax.all_gather(qkv_weight, 'space', axis=0, tiled=True)  108 us
    all_gather x1, waiting for transfers between devices, entering(): everything = lax.all_gather(value.astype(jnp.bfloat16), axis)  44.8 us
    convert_element_type x32, other arithmetic, lap(): new = combine(before, everything[k].astype(value.dtype))  38 us
    all_gather x1, waiting for transfers between devices, per_device(): lax.all_gather(out_weight, 'space', axis=0, tiled=True)  33.7 us
    dot_general x2, matrix products, fold_product(): return jnp.dot(left_side, block_rows, preferred_element_type=jnp.float32)  9.37 us
  transfers between devices with their start and end apart: 6, of which 5 were waited for; matrix products, arithmetic and copies ran while one was open for 12% of the time, Pallas kernels for 0%

commit v1 on v0

v1 whole, which is shorter than its diff:
```python
import jax
import jax.numpy as jnp
from jax import lax
from jax.experimental import pallas as pl
from jax.experimental.pallas import tpu as pltpu
from jax.sharding import PartitionSpec as P

MESH = pl.DeviceIdType.MESH
D = 1152
ROWS = 72
TOKENS = 256
COLS = 64
NZ = 16
TILES = 9
LANES = 128
LAG = 2
LOWEST = -3.0e38
EPS = 1e-06


def kernel(
    tok_ref, qkv_ref, ow_ref, conv_ref, gain_ref, out_ref,
    wkv, wqo, wo, wo_flat, tsib, split, acc, kvb, qb, stage, halo, local,
    part_low, a_in, f_in, b_in, chip_low, c_in, readout, mix,
    zkv_s, zkv_r, zqo_s, zqo_r, kvs_s, kvs_r, qos_s, qos_r,
    tok_sem, kv_sem, q_sem, o_sem, halo_s, halo_r, a_s, a_r, f_sem, b_s, b_r, c_s, c_r,
):
    tm = lax.axis_index("tm")
    z = lax.axis_index("space")
    core = lax.rem(tm, 2)
    chip = tm // 2
    x = chip // 4
    y = lax.rem(chip, 4)

    def at(px, py, pc, pz):
        return ((px * 4 + py) * 2 + pc, pz)

    def x_off(i):
        return at(lax.rem(x + i + 4, 4), y, core, z)

    def y_off(i):
        return at(x, lax.rem(y + i + 4, 4), core, z)

    def z_off(i):
        return at(x, y, core, lax.rem(z + i + NZ, NZ))

    sibling = at(x, y, 1 - core, z)

    def remote(src, dst, ssem, rsem, device):
        return pltpu.make_async_remote_copy(
            src_ref=src, dst_ref=dst, send_sem=ssem, recv_sem=rsem,
            device_id=device, device_id_type=MESH,
        )

    slot_tile = [0, 1 + x, 5 + y]
    slot_tile += [1 + lax.rem(x + i, 4) for i in (1, 2, 3)]
    slot_tile += [5 + lax.rem(y + i, 4) for i in (1, 2, 3)]

    def lanes(slot):
        return pl.ds(slot * LANES, LANES)

    def tile_lanes(tile):
        return pl.ds(pl.multiple_of(tile * LANES, LANES), LANES)

    peers = [z_off(1), z_off(-1), sibling]
    peers += [x_off(i) for i in (1, 2, 3)] + [y_off(i) for i in (1, 2, 3)]
    barrier = pltpu.get_barrier_semaphore()
    for peer in peers:
        pl.semaphore_signal(barrier, inc=1, device_id=peer, device_id_type=MESH)

    for slot in range(TILES):
        tile = slot_tile[slot]
        offset = (1 + core) * TILES + tile
        wkv[z, :, lanes(slot)] = qkv_ref[:, tile_lanes(offset)]

    @pl.when(core == 0)
    def _():
        for slot in range(TILES):
            wqo[z, :, lanes(slot)] = qkv_ref[:, tile_lanes(slot_tile[slot])]

    @pl.when(core == 1)
    def _():
        for slot in range(TILES):
            wqo[z, :, lanes(slot)] = ow_ref[:, tile_lanes(slot_tile[slot])]

    pl.semaphore_wait(barrier, len(peers))

    def z_kv(way, s, t, source):
        ref = wkv.at[source, :, lanes(t)]
        return remote(ref, ref, zkv_s.at[way, s - 1, t], zkv_r.at[way, s - 1, t], z_off(1 - 2 * way))

    def z_qo(way, s, source):
        ref = wqo.at[source, :, pl.ds(0, 3 * LANES)]
        return remote(ref, ref, zqo_s.at[way, s - 1], zqo_r.at[way, s - 1], z_off(1 - 2 * way))

    def share(buf, ssem, rsem, way, s, source, line, i):
        device = x_off(-i) if line == 0 else y_off(-i)
        at_sem = (way, s - 1, 3 * line + i - 1)
        return remote(
            buf.at[source, :, lanes(1 + line)], buf.at[source, :, lanes(2 + 3 * line + i)],
            ssem.at[at_sem], rsem.at[at_sem], device,
        )

    def source_of(way, s):
        return lax.rem(z + NZ - s, NZ) if way == 0 else lax.rem(z + s, NZ)

    for t in range(3):
        for way in range(2):
            z_kv(way, 1, t, z).start()
    token_swap = remote(tok_ref, tsib, tok_sem.at[0], tok_sem.at[1], sibling)
    token_swap.start()
    for way in range(2):
        z_qo(way, 1, z).start()

    for block in range(NZ):
        split[block, 0:TOKENS, :] = tok_ref[:, block * ROWS : (block + 1) * ROWS]
    token_swap.wait()
    for block in range(NZ):
        split[block, TOKENS : 2 * TOKENS, :] = tsib[:, block * ROWS : (block + 1) * ROWS]

    def add_source(buf, source, first):
        left = split[source]
        for n in range(3):
            cols = pl.ds(n * 3 * LANES, 3 * LANES)
            term = jnp.dot(left, buf[source, :, cols], preferred_element_type=jnp.float32)
            acc[:, cols] = term if first else acc[:, cols] + term

    add_source(wkv, z, True)

    def ring(s, carry):
        for way in range(2):
            @pl.when(s <= 8 - way)
            def _():
                source = source_of(way, s)
                for t in (1, 2, 0):
                    z_kv(way, s, t, source).wait_recv()

                    @pl.when(s < 8 - way)
                    def _():
                        z_kv(way, s + 1, t, source).start()

                    if t > 0:
                        for i in (1, 2, 3):
                            share(wkv, kvs_s, kvs_r, way, s, source, t - 1, i).start()

        late = s - LAG
        for way in range(2):
            @pl.when((late >= 1) & (late <= 8 - way))
            def _():
                source = source_of(way, late)
                z_qo(way, late, source).wait_recv()

                @pl.when(late < 8 - way)
                def _():
                    z_qo(way, late + 1, source).start()

                for line in range(2):
                    for i in (1, 2, 3):
                        share(wqo, qos_s, qos_r, way, late, source, line, i).start()

                for line in range(2):
                    for i in (1, 2, 3):
                        share(wkv, kvs_s, kvs_r, way, late, source, line, i).wait_recv()
                add_source(wkv, source, False)

        return carry

    lax.fori_loop(1, 9 + LAG, ring, 0)

    floor = jnp.where(core == 0, 0.0, LOWEST).astype(jnp.float32)
    swaps = []
    for n in range(3):
        for k in range(3):
            slot = 3 * n + k
            stage[n, :, lanes(k)] = jnp.maximum(acc[TOKENS:, lanes(slot)], floor).astype(jnp.bfloat16)
        swap = remote(stage.at[n], stage.at[3 + n], kv_sem.at[n], kv_sem.at[3 + n], sibling)
        swap.start()
        swaps.append(swap)
    for slot in range(TILES):
        kvb[core, :, tile_lanes(slot_tile[slot])] = jnp.maximum(
            acc[0:TOKENS, lanes(slot)], floor
        ).astype(jnp.bfloat16)
    for n in range(3):
        swaps[n].wait()
        for k in range(3):
            slot = 3 * n + k
            kvb[1 - core, :, tile_lanes(slot_tile[slot])] = stage[3 + n, :, lanes(k)]

    down = remote(kvb.at[1, pl.ds(3 * COLS, COLS)], halo.at[0], halo_s.at[0], halo_r.at[0], z_off(1))
    up = remote(kvb.at[1, pl.ds(0, COLS)], halo.at[1], halo_s.at[1], halo_r.at[1], z_off(-1))

    row_head = lax.broadcasted_iota(jnp.int32, (LANES, LANES), 0) // 32
    col_head = lax.broadcasted_iota(jnp.int32, (LANES, LANES), 1) // 32
    same_head = row_head == col_head

    def a_copy(j):
        return remote(part_low.at[j], a_in.at[z], a_s.at[j], a_r.at[z], at(x, y, core, j))

    for j in range(TILES):
        gram = lax.dot_general(
            kvb[0, :, lanes(j)], kvb[1, :, lanes(j)], (((0,), (0,)), ((), ())),
            preferred_element_type=jnp.float32,
        )
        gram = jnp.where(same_head, gram, 0.0)
        part = gram[0:32] + gram[32:64] + gram[64:96] + gram[96:128]
        part_low[j] = part.astype(jnp.bfloat16)

        @pl.when(z != j)
        def _():
            a_copy(j).start()

    @pl.when(z < NZ - 1)
    def _():
        down.start()

    @pl.when(z > 0)
    def _():
        up.start()

    def wait_shares(s, carry):
        for way in range(2):
            @pl.when(s <= 8 - way)
            def _():
                source = source_of(way, s)
                for line in range(2):
                    for i in (1, 2, 3):
                        share(wqo, qos_s, qos_r, way, s, source, line, i).wait_recv()
        return carry

    lax.fori_loop(1, 9, wait_shares, 0)

    o_send = remote(wqo, wo, o_sem.at[0], o_sem.at[1], sibling)
    q_send = remote(qb.at[1], qb.at[0], q_sem.at[0], q_sem.at[1], sibling)

    @pl.when(core == 1)
    def _():
        o_send.start()

    @pl.when(core == 0)
    def _():
        add_source(wqo, 0, True)

        def more(source, carry):
            add_source(wqo, source, False)
            return carry

        lax.fori_loop(1, NZ, more, 0)
        for slot in range(TILES):
            qb[1, :, tile_lanes(slot_tile[slot])] = jnp.maximum(
                acc[TOKENS:, lanes(slot)], 0.0
            ).astype(jnp.bfloat16)
        q_send.start()
        for slot in range(TILES):
            qb[0, :, tile_lanes(slot_tile[slot])] = jnp.maximum(
                acc[0:TOKENS, lanes(slot)], 0.0
            ).astype(jnp.bfloat16)

    def f_copy():
        return remote(f_in.at[0], f_in.at[1], f_sem.at[0], f_sem.at[1], sibling)

    def b_copy(i):
        later = chip + i
        return remote(
            chip_low, b_in.at[i - 1], b_s.at[i - 1], b_r.at[i - 1], (later * 2 + core, z)
        )

    def c_copy(j):
        return remote(c_in.at[z], c_in.at[z], c_s.at[j], c_r.at[z], at(x, y, core, j))

    @pl.when(z < TILES)
    def _():
        f_in[0] = part_low[z].astype(jnp.float32)

        def gather(k, carry):
            source = lax.rem(z + k, NZ)
            remote(part_low.at[0], a_in.at[source], a_s.at[0], a_r.at[source], z_off(1)).wait_recv()
            f_in[0] = f_in[0] + a_in[source].astype(jnp.float32)
            return carry

        lax.fori_loop(1, NZ, gather, 0)
        swap = f_copy()
        swap.start()
        swap.wait()
        chip_low[...] = (f_in[0] + f_in[1]).astype(jnp.bfloat16)
        for i in range(1, NZ):
            @pl.when(chip + i < NZ)
            def _():
                b_copy(i).start()
        readout[0:32, 0:LANES] = f_in[0] + jnp.where(core == 1, f_in[1], 0.0)
        for i in range(1, NZ):
            @pl.when(chip >= i)
            def _():
                b_copy(i).wait_recv()
                readout[0:32, 0:LANES] += b_in[i - 1].astype(jnp.float32)
        c_in[z] = readout[0:32, 0:LANES].astype(jnp.bfloat16)
        for j in range(NZ):
            @pl.when(z != j)
            def _():
                c_copy(j).start()

    @pl.when(z > 0)
    def _():
        down.wait_recv()

    @pl.when(z == 0)
    def _():
        halo[0] = jnp.zeros((COLS, D), jnp.bfloat16)

    @pl.when(z < NZ - 1)
    def _():
        up.wait_recv()

    @pl.when(z == NZ - 1)
    def _():
        halo[1] = jnp.zeros((COLS, D), jnp.bfloat16)

    col = lax.broadcasted_iota(jnp.int32, (COLS, LANES), 0)

    def conv(j, carry):
        cols = tile_lanes(j)
        weight = conv_ref[:, cols]
        sums = [jnp.zeros((COLS, LANES), jnp.float32) for _ in range(4)]
        for row in range(6):
            if row == 0:
                mid = halo[0, :, cols]
            elif row == 5:
                mid = halo[1, :, cols]
            else:
                mid = kvb[1, pl.ds((row - 1) * COLS, COLS), cols]
            mid = mid.astype(jnp.float32)
            left = jnp.where(col == 0, 0.0, pltpu.roll(mid, 1, 0))
            right = jnp.where(col == COLS - 1, 0.0, pltpu.roll(mid, COLS - 1, 0))
            for a in range(3):
                r = row - a
                if 0 <= r < 4:
                    sums[r] = (
                        sums[r] + weight[3 * a] * left + weight[3 * a + 1] * mid
                        + weight[3 * a + 2] * right
                    )
        for r in range(4):
            local[pl.ds(r * COLS, COLS), cols] = sums[r]
        return carry

    lax.fori_loop(0, TILES, conv, 0)

    @pl.when(core == 0)
    def _():
        o_send.wait_recv()

    def flatten(buf):
        def pair(k, carry):
            for slot in range(TILES):
                both = jnp.concatenate(
                    [
                        buf[2 * k, :, lanes(slot)].astype(jnp.float32),
                        buf[2 * k + 1, :, lanes(slot)].astype(jnp.float32),
                    ],
                    axis=0,
                )
                rows = pl.ds(pl.multiple_of(k * 2 * ROWS, 16), 2 * ROWS)
                wo_flat[rows, lanes(slot)] = both.astype(jnp.bfloat16)
            return carry

        lax.fori_loop(0, NZ // 2, pair, 0)

    @pl.when(core == 0)
    def _():
        flatten(wo)

    @pl.when(core == 1)
    def _():
        flatten(wqo)
        q_send.wait_recv()

    for j in range(TILES):
        @pl.when(z != j)
        def _():
            remote(c_in.at[j], c_in.at[j], c_s.at[j], c_r.at[j], z_off(1)).wait_recv()

    square = jnp.zeros((TOKENS, LANES), jnp.float32)
    for j in range(TILES):
        state = jnp.concatenate([c_in[j].astype(jnp.float32)] * 4, axis=0)
        state = jnp.where(same_head, state, 0.0).astype(jnp.bfloat16)
        term = jnp.dot(qb[0, :, lanes(j)], state, preferred_element_type=jnp.float32)
        readout[:, lanes(j)] = term
        square = square + term * term
    mean_square = jnp.sum(square, axis=-1, keepdims=True) * (1.0 / D)
    scale = lax.rsqrt(mean_square + EPS)
    for j in range(TILES):
        normed = readout[:, lanes(j)] * scale * gain_ref[:, lanes(j)]
        mix[:, lanes(j)] = (normed + local[:, lanes(j)]).astype(jnp.bfloat16)
    for n in range(3):
        cols = pl.ds(n * 3 * LANES, 3 * LANES)
        result = jnp.dot(mix[...], wo_flat[:, cols], preferred_element_type=jnp.float32)
        result = result.astype(jnp.bfloat16)
        for k in range(3):
            out_ref[:, tile_lanes(slot_tile[3 * n + k])] = result[:, k * LANES : (k + 1) * LANES]

    def sends(s, carry):
        for way in range(2):
            @pl.when(s <= 8 - way)
            def _():
                source = source_of(way, s)
                for t in range(3):
                    z_kv(way, s, t, source).wait_send()
                z_qo(way, s, source).wait_send()
                for line in range(2):
                    for i in (1, 2, 3):
                        share(wkv, kvs_s, kvs_r, way, s, source, line, i).wait_send()
                        share(wqo, qos_s, qos_r, way, s, source, line, i).wait_send()
        return carry

    lax.fori_loop(1, 9, sends, 0)
    for j in range(TILES):
        @pl.when(z != j)
        def _():
            a_copy(j).wait_send()

    @pl.when(z < NZ - 1)
    def _():
        down.wait_send()

    @pl.when(z > 0)
    def _():
        up.wait_send()

    @pl.when(core == 1)
    def _():
        o_send.wait_send()

    @pl.when(core == 0)
    def _():
        q_send.wait_send()

    @pl.when(z < TILES)
    def _():
        for i in range(1, NZ):
            @pl.when(chip + i < NZ)
            def _():
                b_copy(i).wait_send()
        for j in range(NZ):
            @pl.when(z != j)
            def _():
                c_copy(j).wait_send()


def per_device(video_tokens, qkv_weight, out_weight, conv_weight, norm_gain):
    tokens = video_tokens.reshape(TOKENS, D)
    bf16, f32 = jnp.bfloat16, jnp.float32
    vmem = pl.BlockSpec(memory_space=pltpu.VMEM)
    dma = pltpu.SemaphoreType.DMA
    result = pl.pallas_call(
        kernel,
        out_shape=jax.ShapeDtypeStruct((TOKENS, D), bf16),
        in_specs=[vmem] * 5,
        out_specs=vmem,
        scratch_shapes=[
            pltpu.VMEM((NZ, ROWS, D), bf16),
            pltpu.VMEM((NZ, ROWS, D), bf16),
            pltpu.VMEM((NZ, ROWS, D), bf16),
            pltpu.VMEM((D, D), bf16),
            pltpu.VMEM((TOKENS, D), bf16),
            pltpu.VMEM((NZ, 2 * TOKENS, ROWS), bf16),
            pltpu.VMEM((2 * TOKENS, D), f32),
            pltpu.VMEM((2, TOKENS, D), bf16),
            pltpu.VMEM((2, TOKENS, D), bf16),
            pltpu.VMEM((6, TOKENS, 3 * LANES), bf16),
            pltpu.VMEM((2, COLS, D), bf16),
            pltpu.VMEM((TOKENS, D), f32),
            pltpu.VMEM((TILES, 32, LANES), bf16),
            pltpu.VMEM((NZ, 32, LANES), bf16),
            pltpu.VMEM((2, 32, LANES), f32),
            pltpu.VMEM((NZ - 1, 32, LANES), bf16),
            pltpu.VMEM((32, LANES), bf16),
            pltpu.VMEM((TILES, 32, LANES), bf16),
            pltpu.VMEM((TOKENS, D), f32),
            pltpu.VMEM((TOKENS, D), bf16),
            dma((2, 8, 3)), dma((2, 8, 3)),
            dma((2, 8)), dma((2, 8)),
            dma((2, 8, 6)), dma((2, 8, 6)),
            dma((2, 8, 6)), dma((2, 8, 6)),
            dma((2,)),
            dma((6,)),
            dma((2,)),
            dma((2,)),
            dma((2,)), dma((2,)),
            dma((TILES,)), dma((NZ,)),
            dma((2,)),
            dma((NZ - 1,)), dma((NZ - 1,)),
            dma((NZ,)), dma((TILES,)),
        ],
        compiler_params=pltpu.CompilerParams(
            collective_id=0, has_side_effects=True, vmem_limit_bytes=48 * 2**20
        ),
        name="block",
    )(tokens, qkv_weight, out_weight, conv_weight.reshape(9, D), norm_gain.reshape(1, D))
    return result.reshape(video_tokens.shape)


def solution(mesh):
    in_specs = (P("tm", "space", None, None), P("space", None), P("space", None), P(), P())
    out_specs = P("tm", "space", None, None)
    return jax.shard_map(
        per_device, mesh=mesh, in_specs=in_specs, out_specs=out_specs, check_vma=False
    )
```

time: 408 us -> 89.1 us (0.22)
  the two profiles are of different devices: /device:TPU:30 before, /device:TPU:7 now
where the time goes in v1:
time: 89.1 us; the launch traced here: 87.5 us
  Pallas kernels  82.1 us (92%)
  local copies, waits for them, and re-layouts  5.36 us (6%)
    pallas_call x1, Pallas kernels, per_device(): pl.pallas_call(kernel, out_shape=jax.ShapeDtypeStruct((TOKENS, D), bf16),...  82.1 us
    unnamed x7, local copies, waits for them, and re-layouts  3.82 us

profile of v1, /device:TPU:7, one launch (start us, length us, event | category | flops | bytes accessed | tf_op | source)
XLA Modules:
  0.0 87.5 jit_solution(11928384858419492683)
XLA Ops:
  0.0 0.7 reshape.14.gain_ref
  0.7 0.8 reshape.13.conv_ref
  1.5 0.0 copy-start
  1.6 1.1 %copy-done = bf16[1,4,64,1152]{3,2,1,0:T(8,128)(2,1)S(1)} copy-done((bf16[1,4,64,1152]{3,2,1,0:T(8,128)(2,1)S(1)}, bf16[1,4,64,1152]{3,2,1,0:T(8,128)(2,1)}, u32[]{:S(2)}) %copy-start) | copy-done | bytes 589848
  2.6 0.0 copy-start.1
  2.6 1.0 %copy-done.1 = bf16[72,3456]{1,0:T(8,128)(2,1)S(1)} copy-done((bf16[72,3456]{1,0:T(8,128)(2,1)S(1)}, bf16[72,3456]{1,0:T(8,128)(2,1)}, u32[]{:S(2)}) %copy-start.1) | copy-done | bytes 497688
  3.6 0.0 copy-start.2
  3.6 0.9 %copy-done.2 = bf16[72,1152]{1,0:T(8,128)(2,1)S(1)} copy-done((bf16[72,1152]{1,0:T(8,128)(2,1)S(1)}, bf16[72,1152]{1,0:T(8,128)(2,1)}, u32[]{:S(2)}) %copy-start.2) | copy-done | bytes 165912
  4.6 82.1 %block.1 = bf16[256,1152]{1,0:T(8,128)(2,1)S(1)} custom-call(bf16[256,1152]{1,0:T(8,128)(2,1)S(1)} %bitcast.3, bf16[72,3456]{1,0:T(8,128)(2,1)S(1)} %copy-done.1, bf16[72,1152]{1,0:T(8,128)(2,1)S(1)} %copy-done.2, f32[9,1152]{1,0:T(8,128)S(1)} %reshape.13.conv_ref, f32[1,1152]{1,0:T(1,128)S(1)} %reshape.14.gain_ref), custom_call_target="tpu_custom_call" | custom-call | tf_op jit(solution)/shard_map/block/pallas_call | solution.py:452
  86.6 0.8 copy.7
Async XLA Ops:
  1.5 1.1 %copy-start = (bf16[1,4,64,1152]{3,2,1,0:T(8,128)(2,1)S(1)}, bf16[1,4,64,1152]{3,2,1,0:T(8,128)(2,1)}, u32[]{:S(2)}) copy-start(bf16[1,4,64,1152]{3,2,1,0:T(8,128)(2,1)} %param.5) | copy-start | bytes 1769476
  2.6 1.0 %copy-start.1 = (bf16[72,3456]{1,0:T(8,128)(2,1)S(1)}, bf16[72,3456]{1,0:T(8,128)(2,1)}, u32[]{:S(2)}) copy-start(bf16[72,3456]{1,0:T(8,128)(2,1)} %qkv_ref.1) | copy-start | bytes 1492996
  3.6 0.9 %copy-start.2 = (bf16[72,1152]{1,0:T(8,128)(2,1)S(1)}, bf16[72,1152]{1,0:T(8,128)(2,1)}, u32[]{:S(2)}) copy-start(bf16[72,1152]{1,0:T(8,128)(2,1)} %ow_ref.1) | copy-start | bytes 497668

commit v2 on v1

--- a/solution.py
+++ b/solution.py
@@ -13,17 +13,19 @@
 NZ = 16
 TILES = 9
 LANES = 128
-LAG = 2
+LAG = 1
+QO_START = 1
+QO_LAG = 2
 LOWEST = -3.0e38
 EPS = 1e-06
 
 
 def kernel(
-    tok_ref, qkv_ref, ow_ref, conv_ref, gain_ref, out_ref,
-    wkv, wqo, wo, wo_flat, tsib, split, acc, kvb, qb, stage, halo, local,
-    part_low, a_in, f_in, b_in, chip_low, c_in, readout, mix,
-    zkv_s, zkv_r, zqo_s, zqo_r, kvs_s, kvs_r, qos_s, qos_r,
-    tok_sem, kv_sem, q_sem, o_sem, halo_s, halo_r, a_s, a_r, f_sem, b_s, b_r, c_s, c_r,
+    tok_hbm, qkv_ref, ow_ref, conv_ref, gain_ref, out_ref,
+    wkv, wqo, wo, wo_flat, tok_ref, tsib, split, acc, kvb, qb, stage, halo, local,
+    part_low, a_in, f_sum, b_in, chip_low, c_in, c_out, readout, mix,
+    zkv_s, zkv_r, zqo_s, zqo_r, kvs_s, kvs_r, qos_s, qos_r, load_sem,
+    tok_sem, kv_sem, q_sem, o_sem, halo_s, halo_r, a_s, a_r, b_s, b_r, c_s, c_r,
 ):
     tm = lax.axis_index("tm")
     z = lax.axis_index("space")
@@ -62,36 +64,58 @@
     def tile_lanes(tile):
         return pl.ds(pl.multiple_of(tile * LANES, LANES), LANES)
 
-    peers = [z_off(1), z_off(-1), sibling]
+    peers = [z_off(1), z_off(-1), z_off(2), z_off(-2), sibling]
     peers += [x_off(i) for i in (1, 2, 3)] + [y_off(i) for i in (1, 2, 3)]
     barrier = pltpu.get_barrier_semaphore()
     for peer in peers:
         pl.semaphore_signal(barrier, inc=1, device_id=peer, device_id_type=MESH)
 
+    def load(slot):
+        tile = slot_tile[slot]
+        here = wkv.at[z, :, lanes(slot)]
+        offset = (1 + core) * TILES + tile
+        return pltpu.make_async_copy(qkv_ref.at[:, tile_lanes(offset)], here, load_sem.at[slot])
+
+    def load_qo(slot, origin):
+        here = wqo.at[z, :, lanes(slot)]
+        source = origin.at[:, tile_lanes(slot_tile[slot])]
+        return pltpu.make_async_copy(source, here, load_sem.at[TILES + slot])
+
+    load_tokens = pltpu.make_async_copy(tok_hbm, tok_ref, load_sem.at[2 * TILES])
     for slot in range(TILES):
-        tile = slot_tile[slot]
-        offset = (1 + core) * TILES + tile
-        wkv[z, :, lanes(slot)] = qkv_ref[:, tile_lanes(offset)]
+        load(slot).start()
+    load_tokens.start()
 
     @pl.when(core == 0)
     def _():
         for slot in range(TILES):
-            wqo[z, :, lanes(slot)] = qkv_ref[:, tile_lanes(slot_tile[slot])]
+            load_qo(slot, qkv_ref).start()
 
     @pl.when(core == 1)
     def _():
         for slot in range(TILES):
-            wqo[z, :, lanes(slot)] = ow_ref[:, tile_lanes(slot_tile[slot])]
+            load_qo(slot, ow_ref).start()
+
+    load_tokens.wait()
+    for block in range(NZ):
+        split[block, 0:TOKENS, :] = tok_ref[:, block * ROWS : (block + 1) * ROWS]
+    for slot in range(TILES):
+        load(slot).wait()
+        load_qo(slot, ow_ref).wait()
 
     pl.semaphore_wait(barrier, len(peers))
+
+    def step(way, s):
+        span = 2 - lax.rem(s, 2)
+        return z_off(span if way == 0 else -span)
 
     def z_kv(way, s, t, source):
         ref = wkv.at[source, :, lanes(t)]
-        return remote(ref, ref, zkv_s.at[way, s - 1, t], zkv_r.at[way, s - 1, t], z_off(1 - 2 * way))
+        return remote(ref, ref, zkv_s.at[way, s - 1, t], zkv_r.at[way, s - 1, t], step(way, s))
 
     def z_qo(way, s, source):
         ref = wqo.at[source, :, pl.ds(0, 3 * LANES)]
-        return remote(ref, ref, zqo_s.at[way, s - 1], zqo_r.at[way, s - 1], z_off(1 - 2 * way))
+        return remote(ref, ref, zqo_s.at[way, s - 1], zqo_r.at[way, s - 1], step(way, s))
 
     def share(buf, ssem, rsem, way, s, source, line, i):
         device = x_off(-i) if line == 0 else y_off(-i)
@@ -104,16 +128,14 @@
     def source_of(way, s):
         return lax.rem(z + NZ - s, NZ) if way == 0 else lax.rem(z + s, NZ)
 
-    for t in range(3):
+    for t in (1, 2, 0):
+        for way in range(2):
+            z_kv(way, 2, t, z).start()
+    for t in (1, 2, 0):
         for way in range(2):
             z_kv(way, 1, t, z).start()
     token_swap = remote(tok_ref, tsib, tok_sem.at[0], tok_sem.at[1], sibling)
     token_swap.start()
-    for way in range(2):
-        z_qo(way, 1, z).start()
-
-    for block in range(NZ):
-        split[block, 0:TOKENS, :] = tok_ref[:, block * ROWS : (block + 1) * ROWS]
     token_swap.wait()
     for block in range(NZ):
         split[block, TOKENS : 2 * TOKENS, :] = tsib[:, block * ROWS : (block + 1) * ROWS]
@@ -127,45 +149,66 @@
 
     add_source(wkv, z, True)
 
-    def ring(s, carry):
-        for way in range(2):
-            @pl.when(s <= 8 - way)
-            def _():
-                source = source_of(way, s)
-                for t in (1, 2, 0):
-                    z_kv(way, s, t, source).wait_recv()
-
-                    @pl.when(s < 8 - way)
+    def pass_kv(way, s, source, onward):
+        for t in (1, 2, 0):
+            z_kv(way, s, t, source).wait_recv()
+            if onward:
+                for nxt in (2, 1):
+                    @pl.when(s + nxt <= 8 - way)
                     def _():
-                        z_kv(way, s + 1, t, source).start()
-
-                    if t > 0:
-                        for i in (1, 2, 3):
-                            share(wkv, kvs_s, kvs_r, way, s, source, t - 1, i).start()
-
-        late = s - LAG
-        for way in range(2):
-            @pl.when((late >= 1) & (late <= 8 - way))
-            def _():
-                source = source_of(way, late)
-                z_qo(way, late, source).wait_recv()
-
-                @pl.when(late < 8 - way)
+                        z_kv(way, s + nxt, t, source).start()
+
+        for line in range(2):
+            for i in (1, 2, 3):
+                share(wkv, kvs_s, kvs_r, way, s, source, line, i).start()
+
+    def pass_qo(way, s, source, onward):
+        z_qo(way, s, source).wait_recv()
+        if onward:
+            for nxt in (2, 1):
+                @pl.when(s + nxt <= 8 - way)
                 def _():
-                    z_qo(way, late + 1, source).start()
-
-                for line in range(2):
-                    for i in (1, 2, 3):
-                        share(wqo, qos_s, qos_r, way, late, source, line, i).start()
-
-                for line in range(2):
-                    for i in (1, 2, 3):
-                        share(wkv, kvs_s, kvs_r, way, late, source, line, i).wait_recv()
-                add_source(wkv, source, False)
+                    z_qo(way, s + nxt, source).start()
+        for line in range(2):
+            for i in (1, 2, 3):
+                share(wqo, qos_s, qos_r, way, s, source, line, i).start()
+
+    def take_kv(way, s, source):
+        for line in range(2):
+            for i in (1, 2, 3):
+                share(wkv, kvs_s, kvs_r, way, s, source, line, i).wait_recv()
+        add_source(wkv, source, False)
+
+    def at_place(m, job):
+        for odd in range(2):
+            s = 2 * m - odd
+            for way in range(2):
+                @pl.when((m >= 1) & (s <= 8 - way))
+                def _():
+                    job(way, s, source_of(way, s), odd == 0)
+
+    def ring(m, carry):
+        @pl.when(m <= 4)
+        def _():
+            at_place(m, pass_kv)
+
+        @pl.when(m == QO_START)
+        def _():
+            for nxt in (2, 1):
+                for way in range(2):
+                    z_qo(way, nxt, z).start()
+
+        @pl.when(m > QO_LAG)
+        def _():
+            at_place(m - QO_LAG, pass_qo)
+
+        @pl.when((m > LAG) & (m <= 4 + LAG))
+        def _():
+            at_place(m - LAG, lambda way, s, source, _: take_kv(way, s, source))
 
         return carry
 
-    lax.fori_loop(1, 9 + LAG, ring, 0)
+    lax.fori_loop(1, 5 + QO_LAG, ring, 0)
 
     floor = jnp.where(core == 0, 0.0, LOWEST).astype(jnp.float32)
     swaps = []
@@ -193,8 +236,13 @@
     col_head = lax.broadcasted_iota(jnp.int32, (LANES, LANES), 1) // 32
     same_head = row_head == col_head
 
-    def a_copy(j):
-        return remote(part_low.at[j], a_in.at[z], a_s.at[j], a_r.at[z], at(x, y, core, j))
+    mine = z * 2 + core
+
+    def a_copy(h):
+        return remote(
+            part_low.at[h], a_in.at[core * NZ + z], a_s.at[h], a_r.at[core * NZ + z],
+            at(x, y, h % 2, h // 2),
+        )
 
     for j in range(TILES):
         gram = lax.dot_general(
@@ -203,11 +251,12 @@
         )
         gram = jnp.where(same_head, gram, 0.0)
         part = gram[0:32] + gram[32:64] + gram[64:96] + gram[96:128]
-        part_low[j] = part.astype(jnp.bfloat16)
-
-        @pl.when(z != j)
-        def _():
-            a_copy(j).start()
+        part_low[2 * j] = part[0:16].astype(jnp.bfloat16)
+        part_low[2 * j + 1] = part[16:32].astype(jnp.bfloat16)
+        for h in (2 * j, 2 * j + 1):
+            @pl.when(mine != h)
+            def _():
+                a_copy(h).start()
 
     @pl.when(z < NZ - 1)
     def _():
@@ -255,48 +304,59 @@
                 acc[0:TOKENS, lanes(slot)], 0.0
             ).astype(jnp.bfloat16)
 
-    def f_copy():
-        return remote(f_in.at[0], f_in.at[1], f_sem.at[0], f_sem.at[1], sibling)
-
     def b_copy(i):
         later = chip + i
         return remote(
             chip_low, b_in.at[i - 1], b_s.at[i - 1], b_r.at[i - 1], (later * 2 + core, z)
         )
 
-    def c_copy(j):
-        return remote(c_in.at[z], c_in.at[z], c_s.at[j], c_r.at[z], at(x, y, core, j))
+    def c_copy(pc, k):
+        return remote(
+            c_out.at[pc], c_in.at[mine], c_s.at[pc * NZ + k], c_r.at[mine],
+            at(x, y, pc, lax.rem(z + k, NZ)),
+        )
+
+    far_first = (8, 7, 9, 6, 10, 5, 11, 4, 12, 3, 13, 2, 14, 1, 15)
 
     @pl.when(z < TILES)
     def _():
-        f_in[0] = part_low[z].astype(jnp.float32)
-
-        def gather(k, carry):
-            source = lax.rem(z + k, NZ)
-            remote(part_low.at[0], a_in.at[source], a_s.at[0], a_r.at[source], z_off(1)).wait_recv()
-            f_in[0] = f_in[0] + a_in[source].astype(jnp.float32)
-            return carry
-
-        lax.fori_loop(1, NZ, gather, 0)
-        swap = f_copy()
-        swap.start()
-        swap.wait()
-        chip_low[...] = (f_in[0] + f_in[1]).astype(jnp.bfloat16)
-        for i in range(1, NZ):
+        a_in[core * NZ + z] = part_low[mine]
+        for pc in range(2):
+            f_sum[pc] = jnp.zeros((16, LANES), jnp.float32)
+
+            def gather(k, carry):
+                source = pc * NZ + lax.rem(z + k, NZ)
+
+                @pl.when(source != core * NZ + z)
+                def _():
+                    remote(
+                        part_low.at[0], a_in.at[source], a_s.at[0], a_r.at[source], sibling
+                    ).wait_recv()
+
+                f_sum[pc] = f_sum[pc] + a_in[source].astype(jnp.float32)
+                return carry
+
+            lax.fori_loop(0, NZ, gather, 0)
+        chip_low[...] = (f_sum[0] + f_sum[1]).astype(jnp.bfloat16)
+        for i in range(NZ - 1, 0, -1):
             @pl.when(chip + i < NZ)
             def _():
                 b_copy(i).start()
-        readout[0:32, 0:LANES] = f_in[0] + jnp.where(core == 1, f_in[1], 0.0)
         for i in range(1, NZ):
             @pl.when(chip >= i)
             def _():
                 b_copy(i).wait_recv()
-                readout[0:32, 0:LANES] += b_in[i - 1].astype(jnp.float32)
-        c_in[z] = readout[0:32, 0:LANES].astype(jnp.bfloat16)
-        for j in range(NZ):
-            @pl.when(z != j)
-            def _():
-                c_copy(j).start()
+                f_sum[0] = f_sum[0] + b_in[i - 1].astype(jnp.float32)
+        c_out[0] = f_sum[0].astype(jnp.bfloat16)
+        c_out[1] = (f_sum[0] + f_sum[1]).astype(jnp.bfloat16)
+        c_in[mine] = c_out[core]
+        for k in far_first:
+            for pc in range(2):
+                c_copy(pc, k).start()
+        for pc in range(2):
+            @pl.when(core != pc)
+            def _():
+                c_copy(pc, 0).start()
 
     @pl.when(z > 0)
     def _():
@@ -318,7 +378,7 @@
 
     def conv(j, carry):
         cols = tile_lanes(j)
-        weight = conv_ref[:, cols]
+        weight = [conv_ref[a, :, cols] for a in range(3)]
         sums = [jnp.zeros((COLS, LANES), jnp.float32) for _ in range(4)]
         for row in range(6):
             if row == 0:
@@ -334,8 +394,8 @@
                 r = row - a
                 if 0 <= r < 4:
                     sums[r] = (
-                        sums[r] + weight[3 * a] * left + weight[3 * a + 1] * mid
-                        + weight[3 * a + 2] * right
+                        sums[r] + weight[a][0:1] * left + weight[a][1:2] * mid
+                        + weight[a][2:3] * right
                     )
         for r in range(4):
             local[pl.ds(r * COLS, COLS), cols] = sums[r]
@@ -372,14 +432,15 @@
         flatten(wqo)
         q_send.wait_recv()
 
-    for j in range(TILES):
-        @pl.when(z != j)
+    for h in range(2 * TILES):
+        @pl.when(mine != h)
         def _():
-            remote(c_in.at[j], c_in.at[j], c_s.at[j], c_r.at[j], z_off(1)).wait_recv()
+            remote(c_in.at[h], c_in.at[h], c_s.at[0], c_r.at[h], sibling).wait_recv()
 
     square = jnp.zeros((TOKENS, LANES), jnp.float32)
     for j in range(TILES):
-        state = jnp.concatenate([c_in[j].astype(jnp.float32)] * 4, axis=0)
+        halves = [c_in[2 * j].astype(jnp.float32), c_in[2 * j + 1].astype(jnp.float32)]
+        state = jnp.concatenate(halves * 4, axis=0)
         state = jnp.where(same_head, state, 0.0).astype(jnp.bfloat16)
         term = jnp.dot(qb[0, :, lanes(j)], state, preferred_element_type=jnp.float32)
         readout[:, lanes(j)] = term
@@ -411,10 +472,10 @@
         return carry
 
     lax.fori_loop(1, 9, sends, 0)
-    for j in range(TILES):
-        @pl.when(z != j)
+    for h in range(2 * TILES):
+        @pl.when(mine != h)
         def _():
-            a_copy(j).wait_send()
+            a_copy(h).wait_send()
 
     @pl.when(z < NZ - 1)
     def _():
@@ -438,27 +499,32 @@
             @pl.when(chip + i < NZ)
             def _():
                 b_copy(i).wait_send()
-        for j in range(NZ):
-            @pl.when(z != j)
-            def _():
-                c_copy(j).wait_send()
+        for k in far_first:
+            for pc in range(2):
+                c_copy(pc, k).wait_send()
+        for pc in range(2):
+            @pl.when(core != pc)
+            def _():
+                c_copy(pc, 0).wait_send()
 
 
 def per_device(video_tokens, qkv_weight, out_weight, conv_weight, norm_gain):
     tokens = video_tokens.reshape(TOKENS, D)
     bf16, f32 = jnp.bfloat16, jnp.float32
     vmem = pl.BlockSpec(memory_space=pltpu.VMEM)
+    hbm = pl.BlockSpec(memory_space=pltpu.HBM)
     dma = pltpu.SemaphoreType.DMA
     result = pl.pallas_call(
         kernel,
         out_shape=jax.ShapeDtypeStruct((TOKENS, D), bf16),
-        in_specs=[vmem] * 5,
+        in_specs=[hbm] * 3 + [vmem] * 2,
         out_specs=vmem,
         scratch_shapes=[
             pltpu.VMEM((NZ, ROWS, D), bf16),
             pltpu.VMEM((NZ, ROWS, D), bf16),
             pltpu.VMEM((NZ, ROWS, D), bf16),
             pltpu.VMEM((D, D), bf16),
+            pltpu.VMEM((TOKENS, D), bf16),
             pltpu.VMEM((TOKENS, D), bf16),
             pltpu.VMEM((NZ, 2 * TOKENS, ROWS), bf16),
             pltpu.VMEM((2 * TOKENS, D), f32),
@@ -467,33 +533,34 @@
             pltpu.VMEM((6, TOKENS, 3 * LANES), bf16),
             pltpu.VMEM((2, COLS, D), bf16),
             pltpu.VMEM((TOKENS, D), f32),
-            pltpu.VMEM((TILES, 32, LANES), bf16),
-            pltpu.VMEM((NZ, 32, LANES), bf16),
-            pltpu.VMEM((2, 32, LANES), f32),
-            pltpu.VMEM((NZ - 1, 32, LANES), bf16),
-            pltpu.VMEM((32, LANES), bf16),
-            pltpu.VMEM((TILES, 32, LANES), bf16),
+            pltpu.VMEM((2 * TILES, 16, LANES), bf16),
+            pltpu.VMEM((2 * NZ, 16, LANES), bf16),
+            pltpu.VMEM((2, 16, LANES), f32),
+            pltpu.VMEM((NZ - 1, 16, LANES), bf16),
+            pltpu.VMEM((16, LANES), bf16),
+            pltpu.VMEM((2 * TILES, 16, LANES), bf16),
+            pltpu.VMEM((2, 16, LANES), bf16),
             pltpu.VMEM((TOKENS, D), f32),
             pltpu.VMEM((TOKENS, D), bf16),
             dma((2, 8, 3)), dma((2, 8, 3)),
             dma((2, 8)), dma((2, 8)),
             dma((2, 8, 6)), dma((2, 8, 6)),
             dma((2, 8, 6)), dma((2, 8, 6)),
+            dma((2 * TILES + 1,)),
             dma((2,)),
             dma((6,)),
             dma((2,)),
             dma((2,)),
             dma((2,)), dma((2,)),
-            dma((TILES,)), dma((NZ,)),
-            dma((2,)),
+            dma((2 * TILES,)), dma((2 * NZ,)),
             dma((NZ - 1,)), dma((NZ - 1,)),
-            dma((NZ,)), dma((TILES,)),
+            dma((2 * NZ,)), dma((2 * TILES,)),
         ],
         compiler_params=pltpu.CompilerParams(
             collective_id=0, has_side_effects=True, vmem_limit_bytes=48 * 2**20
         ),
         name="block",
-    )(tokens, qkv_weight, out_weight, conv_weight.reshape(9, D), norm_gain.reshape(1, D))
+    )(tokens, qkv_weight, out_weight, conv_weight, norm_gain.reshape(1, D))
     return result.reshape(video_tokens.shape)
 
 

time: 89.1 us -> 84.2 us (0.945); the launches traced: 87.5 us -> 83.7 us
  Pallas kernels: 82.1 us -> 78.4 us
    pallas_call x1, Pallas kernels: 82.1 us -> 78.4 us  [per_device(): pl.pallas_call(kernel, out_shape=jax.ShapeDtypeStruct((TOKENS, D), bf16),...]
    unnamed x7 -> x9, local copies, waits for them, and re-layouts: 3.82 us -> 4.64 us
where the time goes in v2:
time: 84.2 us; the launch traced here: 83.7 us
  Pallas kernels  78.4 us (93%)
  local copies, waits for them, and re-layouts  5.34 us (6%)
    pallas_call x1, Pallas kernels, per_device(): pl.pallas_call(kernel, out_shape=jax.ShapeDtypeStruct((TOKENS, D), bf16),...  78.4 us
    unnamed x9, local copies, waits for them, and re-layouts  4.64 us

profile of v2, /device:TPU:7, one launch (start us, length us, event | category | flops | bytes accessed | tf_op | source)
XLA Modules:
  0.0 83.7 jit_solution(11244157008559734728)
XLA Ops:
  0.0 0.7 reshape.10.gain_ref
  0.7 0.0 copy-start
  0.7 1.1 %copy-done = bf16[1,4,64,1152]{3,2,1,0:T(8,128)(2,1)S(1)} copy-done((bf16[1,4,64,1152]{3,2,1,0:T(8,128)(2,1)S(1)}, bf16[1,4,64,1152]{3,2,1,0:T(8,128)(2,1)}, u32[]{:S(2)}) %copy-start) | copy-done | bytes 589848
  1.8 0.0 copy-start.1
  1.8 1.0 %copy-done.1 = bf16[72,3456]{1,0:T(8,128)(2,1)S(1)} copy-done((bf16[72,3456]{1,0:T(8,128)(2,1)S(1)}, bf16[72,3456]{1,0:T(8,128)(2,1)}, u32[]{:S(2)}) %copy-start.1) | copy-done | bytes 497688
  2.8 0.0 copy-start.2
  2.8 0.9 %copy-done.2 = bf16[72,1152]{1,0:T(8,128)(2,1)S(1)} copy-done((bf16[72,1152]{1,0:T(8,128)(2,1)S(1)}, bf16[72,1152]{1,0:T(8,128)(2,1)}, u32[]{:S(2)}) %copy-start.2) | copy-done | bytes 165912
  3.7 0.0 copy-start.3
  3.7 0.8 copy-done.3
  4.5 78.4 %block.1 = bf16[256,1152]{1,0:T(8,128)(2,1)S(1)} custom-call(bf16[256,1152]{1,0:T(8,128)(2,1)S(1)} %bitcast.3, bf16[72,3456]{1,0:T(8,128)(2,1)S(1)} %copy-done.1, bf16[72,1152]{1,0:T(8,128)(2,1)S(1)} %copy-done.2, f32[3,3,1152]{2,1,0:T(4,128)S(1)} %copy-done.3, f32[1,1152]{1,0:T(1,128)S(1)} %reshape.10.gain_ref), custom_call_target="tpu_custom_call" | custom-call | tf_op jit(solution)/shard_map/block/pallas_call | solution.py:517
  82.9 0.8 copy.7
Async XLA Ops:
  0.7 1.1 %copy-start = (bf16[1,4,64,1152]{3,2,1,0:T(8,128)(2,1)S(1)}, bf16[1,4,64,1152]{3,2,1,0:T(8,128)(2,1)}, u32[]{:S(2)}) copy-start(bf16[1,4,64,1152]{3,2,1,0:T(8,128)(2,1)} %param.5) | copy-start | bytes 1769476
  1.8 1.0 %copy-start.1 = (bf16[72,3456]{1,0:T(8,128)(2,1)S(1)}, bf16[72,3456]{1,0:T(8,128)(2,1)}, u32[]{:S(2)}) copy-start(bf16[72,3456]{1,0:T(8,128)(2,1)} %qkv_ref.1) | copy-start | bytes 1492996
  2.8 0.9 %copy-start.2 = (bf16[72,1152]{1,0:T(8,128)(2,1)S(1)}, bf16[72,1152]{1,0:T(8,128)(2,1)}, u32[]{:S(2)}) copy-start(bf16[72,1152]{1,0:T(8,128)(2,1)} %ow_ref.1) | copy-start | bytes 497668
  3.7 0.8 copy-start.3

commit v3 on v2

v3 whole, which is shorter than its diff:
```python
import jax
import jax.numpy as jnp
from jax import lax
from jax.experimental import pallas as pl
from jax.experimental.pallas import tpu as pltpu
from jax.sharding import PartitionSpec as P

MESH = pl.DeviceIdType.MESH
D = 1152
ROWS = 72
TOKENS = 256
COLS = 64
NZ = 16
TILES = 9
LANES = 128
QO_START = 2
QO_FIRST = 4
P2 = 0
P3 = 1
P4 = 2
T1 = 3
T2 = 4
LOWEST = -3.0e38
EPS = 1e-06


def kernel(
    tok_hbm, qkv_ref, ow_ref, conv_hbm, gain_ref, out_ref,
    wkv, wqo, wo, wo_flat, conv_ref, tok_ref, tsib, split, acc, kvb, qb, stage, halo, local,
    part_low, a_in, f_sum, b_in, chip_low, c_in, c_out, readout, mix,
    zkv_r, zqo_r, kvs_r, qos_r, kv_s, qo_s, load_sem,
    tok_sem, kv_sem, q_sem, o_sem, halo_s, halo_r, a_s, a_r, b_s, b_r, c_s, c_r,
):
    tm = lax.axis_index("tm")
    z = lax.axis_index("space")
    core = lax.rem(tm, 2)
    chip = tm // 2
    x = chip // 4
    y = lax.rem(chip, 4)

    def at(px, py, pc, pz):
        return ((px * 4 + py) * 2 + pc, pz)

    def x_off(i):
        return at(lax.rem(x + i + 4, 4), y, core, z)

    def y_off(i):
        return at(x, lax.rem(y + i + 4, 4), core, z)

    def z_off(i):
        return at(x, y, core, lax.rem(z + i + NZ, NZ))

    sibling = at(x, y, 1 - core, z)

    def remote(src, dst, ssem, rsem, device):
        return pltpu.make_async_remote_copy(
            src_ref=src, dst_ref=dst, send_sem=ssem, recv_sem=rsem,
            device_id=device, device_id_type=MESH,
        )

    slot_tile = [0, 1 + x, 5 + y]
    slot_tile += [1 + lax.rem(x + i, 4) for i in (1, 2, 3)]
    slot_tile += [5 + lax.rem(y + i, 4) for i in (1, 2, 3)]

    def lanes(slot):
        return pl.ds(slot * LANES, LANES)

    def tile_lanes(tile):
        return pl.ds(pl.multiple_of(tile * LANES, LANES), LANES)

    peers = [z_off(1), z_off(-1), z_off(2), z_off(-2), sibling]
    peers += [x_off(i) for i in (1, 2, 3)] + [y_off(i) for i in (1, 2, 3)]
    barrier = pltpu.get_barrier_semaphore()
    for peer in peers:
        pl.semaphore_signal(barrier, inc=1, device_id=peer, device_id_type=MESH)

    def load(slot):
        tile = slot_tile[slot]
        here = wkv.at[z, :, lanes(slot)]
        offset = (1 + core) * TILES + tile
        return pltpu.make_async_copy(qkv_ref.at[:, tile_lanes(offset)], here, load_sem.at[0])

    def load_qo(slot, origin):
        here = wqo.at[z, :, lanes(slot)]
        source = origin.at[:, tile_lanes(slot_tile[slot])]
        return pltpu.make_async_copy(source, here, load_sem.at[1])

    load_tokens = pltpu.make_async_copy(tok_hbm, tok_ref, load_sem.at[2])
    for slot in range(TILES):
        load(slot).start()
    load_tokens.start()

    @pl.when(core == 0)
    def _():
        for slot in range(TILES):
            load_qo(slot, qkv_ref).start()

    @pl.when(core == 1)
    def _():
        for slot in range(TILES):
            load_qo(slot, ow_ref).start()

    load_conv = pltpu.make_async_copy(conv_hbm, conv_ref, load_sem.at[3])
    load_conv.start()

    def local_wait(ref, sem):
        pltpu.make_async_copy(ref, ref, sem).wait()

    local_wait(wkv.at[z], load_sem.at[0])
    load_tokens.wait()
    pl.semaphore_wait(barrier, len(peers))

    def step(way, s):
        span = 2 - lax.rem(s, 2)
        return z_off(span if way == 0 else -span)

    def z_kv(way, s, t, source):
        ref = wkv.at[source, :, lanes(t)]
        return remote(ref, ref, kv_s.at[0], zkv_r.at[way, s - 1, t], step(way, s))

    def z_qo(way, s, source):
        ref = wqo.at[source, :, pl.ds(0, 3 * LANES)]
        return remote(ref, ref, qo_s.at[0], zqo_r.at[way, s - 1], step(way, s))

    def share(buf, ssem, rsem, source, line, i):
        return remote(
            buf.at[source, :, lanes(1 + line)], buf.at[source, :, lanes(2 + 3 * line + i)],
            ssem, rsem, x_off(-i) if line == 0 else y_off(-i),
        )

    def share_all(buf, ssem, rsem, source):
        for i in (2, 1, 3):
            for line in range(2):
                share(buf, ssem, rsem, source, line, i).start()

    def source_of(way, s):
        return lax.rem(z + NZ - s, NZ) if way == 0 else lax.rem(z + s, NZ)

    for s in (2, 1):
        for t in (1, 2, 0):
            for way in range(2):
                z_kv(way, s, t, z).start()
    token_swap = remote(tok_ref, tsib, tok_sem.at[0], tok_sem.at[1], sibling)
    token_swap.start()
    for block in range(NZ):
        split[block, 0:TOKENS, :] = tok_ref[:, block * ROWS : (block + 1) * ROWS]
    token_swap.wait()
    for block in range(NZ):
        split[block, TOKENS : 2 * TOKENS, :] = tsib[:, block * ROWS : (block + 1) * ROWS]

    def add_source(buf, source, first):
        left = split[source]
        for n in range(3):
            cols = pl.ds(n * 3 * LANES, 3 * LANES)
            term = jnp.dot(left, buf[source, :, cols], preferred_element_type=jnp.float32)
            acc[:, cols] = term if first else acc[:, cols] + term

    add_source(wkv, z, True)

    def pass_kv(m):
        s = 2 * m
        for t in (1, 2, 0):
            for way in range(2):
                @pl.when(s <= 8 - way)
                def _():
                    z_kv(way, s, t, source_of(way, s)).wait_recv()

                @pl.when(s + 2 <= 8 - way)
                def _():
                    z_kv(way, s + 2, t, source_of(way, s)).start()

        for t in (1, 2, 0):
            for way in range(2):
                @pl.when(s + 1 <= 8 - way)
                def _():
                    z_kv(way, s + 1, t, source_of(way, s)).start()

        for odd in range(2):
            for way in range(2):
                @pl.when(s - odd <= 8 - way)
                def _():
                    source = source_of(way, s - odd)
                    if odd:
                        for t in (1, 2, 0):
                            z_kv(way, s - 1, t, source).wait_recv()
                    share_all(wkv, kv_s.at[0], kvs_r.at[way, s - odd - 1], source)

    def take_kv(m):
        for odd in (1, 0):
            s = 2 * m - odd
            for way in range(2):
                @pl.when(s <= 8 - way)
                def _():
                    source = source_of(way, s)
                    shared = wkv.at[source, :, pl.ds(3 * LANES, 6 * LANES)]
                    remote(shared, shared, kv_s.at[0], kvs_r.at[way, s - 1], sibling).wait_recv()
                    add_source(wkv, source, False)

    def start_qo():
        local_wait(wqo.at[z], load_sem.at[1])
        for s in (2, 1):
            for way in range(2):
                z_qo(way, s, z).start()

    def pass_qo(m):
        for odd in range(2):
            s = 2 * m - odd
            for way in range(2):
                @pl.when(s <= 8 - way)
                def _():
                    source = source_of(way, s)
                    z_qo(way, s, source).wait_recv()
                    if odd == 0:
                        for nxt in (2, 1):
                            @pl.when(s + nxt <= 8 - way)
                            def _():
                                z_qo(way, s + nxt, source).start()

                    share_all(wqo, qo_s.at[0], qos_r.at[m - 1], source)

    def ring(m, carry):
        @pl.when(m <= 4)
        def _():
            pass_kv(m)

        @pl.when(m == QO_START)
        def _():
            start_qo()

        @pl.when(m == QO_FIRST)
        def _():
            pass_qo(1)

        @pl.when(m > 1)
        def _():
            take_kv(m - 1)

        return carry

    def o_copy(source):
        return remote(wqo.at[source], wo.at[source], o_sem.at[0], o_sem.at[1], sibling)

    q_send = remote(qb.at[1], qb.at[0], q_sem.at[0], q_sem.at[1], sibling)

    def use_qo(source, first):
        @pl.when(core == 0)
        def _():
            add_source(wqo, source, first)

        @pl.when(core == 1)
        def _():
            o_copy(source).start()

    def take_qo(m):
        shared = wqo.at[0 : (3 if m == 4 else 4), :, pl.ds(0, 6 * LANES)]
        remote(shared, shared, qo_s.at[0], qos_r.at[m - 1], sibling).wait_recv()

        def one(k, carry):
            s = 2 * m - k // 2
            source = jnp.where(lax.rem(k, 2) == 0, source_of(0, s), source_of(1, s))

            @pl.when((lax.rem(k, 2) == 0) | (s <= 7))
            def _():
                use_qo(source, False)

            return carry

        lax.fori_loop(0, 4, one, 0)

    def hook(place):
        for m, passed in ((2, P2), (3, P3), (4, P4)):
            if passed == place:
                pass_qo(m)
        for m, taken in ((1, T1), (2, T2)):
            if taken == place:
                if m == 1:
                    use_qo(z, True)
                take_qo(m)

    lax.fori_loop(1, 6, ring, 0)
    hook(0)

    floor = jnp.where(core == 0, 0.0, LOWEST).astype(jnp.float32)
    swaps = []
    for n in range(3):
        for k in range(3):
            slot = 3 * n + k
            stage[n, :, lanes(k)] = jnp.maximum(acc[TOKENS:, lanes(slot)], floor).astype(jnp.bfloat16)
        swap = remote(stage.at[n], stage.at[3 + n], kv_sem.at[n], kv_sem.at[3 + n], sibling)
        swap.start()
        swaps.append(swap)
    for slot in range(TILES):
        kvb[core, :, tile_lanes(slot_tile[slot])] = jnp.maximum(
            acc[0:TOKENS, lanes(slot)], floor
        ).astype(jnp.bfloat16)
    for n in range(3):
        swaps[n].wait()
        for k in range(3):
            slot = 3 * n + k
            kvb[1 - core, :, tile_lanes(slot_tile[slot])] = stage[3 + n, :, lanes(k)]

    down = remote(kvb.at[1, pl.ds(3 * COLS, COLS)], halo.at[0], halo_s.at[0], halo_r.at[0], z_off(1))
    up = remote(kvb.at[1, pl.ds(0, COLS)], halo.at[1], halo_s.at[1], halo_r.at[1], z_off(-1))

    row_head = lax.broadcasted_iota(jnp.int32, (LANES, LANES), 0) // 32
    col_head = lax.broadcasted_iota(jnp.int32, (LANES, LANES), 1) // 32
    same_head = row_head == col_head

    mine = z * 2 + core

    def a_copy(h):
        return remote(
            part_low.at[h], a_in.at[core * NZ + z], a_s.at[0], a_r.at[0],
            at(x, y, h % 2, h // 2),
        )

    for j in range(TILES):
        gram = lax.dot_general(
            kvb[0, :, lanes(j)], kvb[1, :, lanes(j)], (((0,), (0,)), ((), ())),
            preferred_element_type=jnp.float32,
        )
        gram = jnp.where(same_head, gram, 0.0)
        part = gram[0:32] + gram[32:64] + gram[64:96] + gram[96:128]
        part_low[2 * j] = part[0:16].astype(jnp.bfloat16)
        part_low[2 * j + 1] = part[16:32].astype(jnp.bfloat16)
        for h in (2 * j, 2 * j + 1):
            @pl.when(mine != h)
            def _():
                a_copy(h).start()

    @pl.when(z < NZ - 1)
    def _():
        down.start()

    @pl.when(z > 0)
    def _():
        up.start()

    hook(1)

    @pl.when(z > 0)
    def _():
        down.wait_recv()

    @pl.when(z == 0)
    def _():
        halo[0] = jnp.zeros((COLS, D), jnp.bfloat16)

    @pl.when(z < NZ - 1)
    def _():
        up.wait_recv()

    @pl.when(z == NZ - 1)
    def _():
        halo[1] = jnp.zeros((COLS, D), jnp.bfloat16)

    load_conv.wait()
    col = lax.broadcasted_iota(jnp.int32, (COLS, LANES), 0)

    def conv(j, carry):
        cols = tile_lanes(j)
        weight = [conv_ref[a, :, cols] for a in range(3)]
        sums = [jnp.zeros((COLS, LANES), jnp.float32) for _ in range(4)]
        for row in range(6):
            if row == 0:
                mid = halo[0, :, cols]
            elif row == 5:
                mid = halo[1, :, cols]
            else:
                mid = kvb[1, pl.ds((row - 1) * COLS, COLS), cols]
            mid = mid.astype(jnp.float32)
            left = jnp.where(col == 0, 0.0, pltpu.roll(mid, 1, 0))
            right = jnp.where(col == COLS - 1, 0.0, pltpu.roll(mid, COLS - 1, 0))
            for a in range(3):
                r = row - a
                if 0 <= r < 4:
                    sums[r] = (
                        sums[r] + weight[a][0:1] * left + weight[a][1:2] * mid
                        + weight[a][2:3] * right
                    )
        for r in range(4):
            local[pl.ds(r * COLS, COLS), cols] = sums[r]
        return carry

    lax.fori_loop(0, TILES, conv, 0)

    hook(2)

    def b_copy(i):
        later = chip + i
        return remote(chip_low, b_in.at[i - 1], b_s.at[0], b_r.at[0], (later * 2 + core, z))

    def c_copy(pc, k):
        return remote(
            c_out.at[pc], c_in.at[mine], c_s.at[0], c_r.at[0], at(x, y, pc, lax.rem(z + k, NZ))
        )

    far_first = (8, 7, 9, 6, 10, 5, 11, 4, 12, 3, 13, 2, 14, 1, 15)

    @pl.when(z < TILES)
    def _():
        a_in[core * NZ + z] = part_low[mine]
        others = a_in.at[0 : 2 * NZ - 1]
        remote(others, others, a_s.at[0], a_r.at[0], sibling).wait_recv()
        for pc in range(2):
            f_sum[pc] = jnp.sum(a_in[pc * NZ : (pc + 1) * NZ].astype(jnp.float32), axis=0)
        chip_low[...] = (f_sum[0] + f_sum[1]).astype(jnp.bfloat16)
        for i in range(NZ - 1, 0, -1):
            @pl.when(chip + i < NZ)
            def _():
                b_copy(i).start()

    hook(3)

    @pl.when(z < TILES)
    def _():
        for n in range(1, NZ):
            @pl.when(chip == n)
            def _():
                earlier = b_in.at[0:n]
                remote(earlier, earlier, b_s.at[0], b_r.at[0], sibling).wait_recv()
                f_sum[0] = f_sum[0] + jnp.sum(b_in[0:n].astype(jnp.float32), axis=0)

        c_out[0] = f_sum[0].astype(jnp.bfloat16)
        c_out[1] = (f_sum[0] + f_sum[1]).astype(jnp.bfloat16)
        c_in[mine] = c_out[core]
        for k in far_first:
            for pc in range(2):
                c_copy(pc, k).start()
        for pc in range(2):
            @pl.when(core != pc)
            def _():
                c_copy(pc, 0).start()

    hook(4)
    take_qo(3)
    take_qo(4)

    @pl.when(core == 0)
    def _():
        for slot in range(TILES):
            qb[1, :, tile_lanes(slot_tile[slot])] = jnp.maximum(
                acc[TOKENS:, lanes(slot)], 0.0
            ).astype(jnp.bfloat16)
        q_send.start()
        for slot in range(TILES):
            qb[0, :, tile_lanes(slot_tile[slot])] = jnp.maximum(
                acc[0:TOKENS, lanes(slot)], 0.0
            ).astype(jnp.bfloat16)

    @pl.when(core == 0)
    def _():
        remote(wo, wo, o_sem.at[0], o_sem.at[1], sibling).wait_recv()

    def flatten(buf):
        def pair(k, carry):
            for slot in range(TILES):
                both = jnp.concatenate(
                    [
                        buf[2 * k, :, lanes(slot)].astype(jnp.float32),
                        buf[2 * k + 1, :, lanes(slot)].astype(jnp.float32),
                    ],
                    axis=0,
                )
                rows = pl.ds(pl.multiple_of(k * 2 * ROWS, 16), 2 * ROWS)
                wo_flat[rows, lanes(slot)] = both.astype(jnp.bfloat16)
            return carry

        lax.fori_loop(0, NZ // 2, pair, 0)

    @pl.when(core == 0)
    def _():
        flatten(wo)

    @pl.when(core == 1)
    def _():
        flatten(wqo)
        q_send.wait_recv()

    owner = z < TILES

    def wait_c(count):
        rest = c_in.at[0:count]
        remote(rest, rest, c_s.at[0], c_r.at[0], sibling).wait_recv()

    @pl.when(owner)
    def _():
        wait_c(2 * TILES - 1)

    @pl.when(jnp.logical_not(owner))
    def _():
        wait_c(2 * TILES)

    square = jnp.zeros((TOKENS, LANES), jnp.float32)
    for j in range(TILES):
        halves = [c_in[2 * j].astype(jnp.float32), c_in[2 * j + 1].astype(jnp.float32)]
        state = jnp.concatenate(halves * 4, axis=0)
        state = jnp.where(same_head, state, 0.0).astype(jnp.bfloat16)
        term = jnp.dot(qb[0, :, lanes(j)], state, preferred_element_type=jnp.float32)
        readout[:, lanes(j)] = term
        square = square + term * term
    mean_square = jnp.sum(square, axis=-1, keepdims=True) * (1.0 / D)
    scale = lax.rsqrt(mean_square + EPS)
    for j in range(TILES):
        normed = readout[:, lanes(j)] * scale * gain_ref[lanes(j)].reshape(1, LANES)
        mix[:, lanes(j)] = (normed + local[:, lanes(j)]).astype(jnp.bfloat16)
    for n in range(3):
        cols = pl.ds(n * 3 * LANES, 3 * LANES)
        result = jnp.dot(mix[...], wo_flat[:, cols], preferred_element_type=jnp.float32)
        result = result.astype(jnp.bfloat16)
        for k in range(3):
            out_ref[:, tile_lanes(slot_tile[3 * n + k])] = result[:, k * LANES : (k + 1) * LANES]

    def sent(ref, sem):
        remote(ref, ref, sem, sem, sibling).wait_send()

    sent(wkv.at[0:15], kv_s.at[0])
    sent(wqo.at[0:15], qo_s.at[0])

    @pl.when(owner)
    def _():
        sent(part_low.at[0 : 2 * TILES - 1], a_s.at[0])
        sent(a_in.at[0 : 2 * NZ - 1], c_s.at[0])
        for n in range(1, NZ):
            @pl.when(chip + n == NZ - 1)
            def _():
                sent(b_in.at[0:n], b_s.at[0])

    @pl.when(jnp.logical_not(owner))
    def _():
        sent(part_low, a_s.at[0])

    @pl.when(z < NZ - 1)
    def _():
        down.wait_send()

    @pl.when(z > 0)
    def _():
        up.wait_send()

    @pl.when(core == 1)
    def _():
        sent(wqo, o_sem.at[0])

    @pl.when(core == 0)
    def _():
        q_send.wait_send()


def per_device(video_tokens, qkv_weight, out_weight, conv_weight, norm_gain):
    tokens = video_tokens.reshape(TOKENS, D)
    bf16, f32 = jnp.bfloat16, jnp.float32
    vmem = pl.BlockSpec(memory_space=pltpu.VMEM)
    hbm = pl.BlockSpec(memory_space=pltpu.HBM)
    dma = pltpu.SemaphoreType.DMA
    result = pl.pallas_call(
        kernel,
        out_shape=jax.ShapeDtypeStruct((TOKENS, D), bf16),
        in_specs=[hbm] * 4 + [vmem],
        out_specs=vmem,
        scratch_shapes=[
            pltpu.VMEM((NZ, ROWS, D), bf16),
            pltpu.VMEM((NZ, ROWS, D), bf16),
            pltpu.VMEM((NZ, ROWS, D), bf16),
            pltpu.VMEM((D, D), bf16),
            pltpu.VMEM((3, 3, D), f32),
            pltpu.VMEM((TOKENS, D), bf16),
            pltpu.VMEM((TOKENS, D), bf16),
            pltpu.VMEM((NZ, 2 * TOKENS, ROWS), bf16),
            pltpu.VMEM((2 * TOKENS, D), f32),
            pltpu.VMEM((2, TOKENS, D), bf16),
            pltpu.VMEM((2, TOKENS, D), bf16),
            pltpu.VMEM((6, TOKENS, 3 * LANES), bf16),
            pltpu.VMEM((2, COLS, D), bf16),
            pltpu.VMEM((TOKENS, D), f32),
            pltpu.VMEM((2 * TILES, 16, LANES), bf16),
            pltpu.VMEM((2 * NZ, 16, LANES), bf16),
            pltpu.VMEM((2, 16, LANES), f32),
            pltpu.VMEM((NZ - 1, 16, LANES), bf16),
            pltpu.VMEM((16, LANES), bf16),
            pltpu.VMEM((2 * TILES, 16, LANES), bf16),
            pltpu.VMEM((2, 16, LANES), bf16),
            pltpu.VMEM((TOKENS, D), f32),
            pltpu.VMEM((TOKENS, D), bf16),
            dma((2, 8, 3)), dma((2, 8)), dma((2, 8)), dma((4,)),
            dma((1,)), dma((1,)), dma((4,)),
            dma((2,)), dma((6,)), dma((2,)), dma((2,)),
            dma((2,)), dma((2,)),
            dma((1,)), dma((1,)), dma((1,)), dma((1,)), dma((1,)), dma((1,)),
        ],
        compiler_params=pltpu.CompilerParams(
            collective_id=0, has_side_effects=True, vmem_limit_bytes=63 * 2**20
        ),
        name="block",
    )(tokens, qkv_weight, out_weight, conv_weight, norm_gain)
    return result.reshape(video_tokens.shape)


def solution(mesh):
    in_specs = (P("tm", "space", None, None), P("space", None), P("space", None), P(), P())
    out_specs = P("tm", "space", None, None)
    return jax.shard_map(
        per_device, mesh=mesh, in_specs=in_specs, out_specs=out_specs, check_vma=False
    )
```

time: 84.2 us -> 74.2 us (0.88)
  Pallas kernels: 78.4 us -> 72.1 us
  local copies, waits for them, and re-layouts: 5.34 us -> 1.92 us
    pallas_call x1, Pallas kernels: 78.4 us -> 72.1 us  [per_device(): pl.pallas_call(kernel, out_shape=jax.ShapeDtypeStruct((TOKENS, D), bf16),...]
    unnamed x9 -> x1, local copies, waits for them, and re-layouts: 4.64 us -> 1.92 us
where the time goes in v3:
time: 74.2 us; the launch traced here: 74 us
  Pallas kernels  72.1 us (97%)
  local copies, waits for them, and re-layouts  1.92 us (3%)
    pallas_call x1, Pallas kernels, per_device(): pl.pallas_call(kernel, out_shape=jax.ShapeDtypeStruct((TOKENS, D), bf16),...  72.1 us
    unnamed x1, local copies, waits for them, and re-layouts  1.92 us

profile of v3, /device:TPU:7, one launch (start us, length us, event | category | flops | bytes accessed | tf_op | source)
XLA Modules:
  0.0 74.0 jit_solution(10427124936702233146)
XLA Ops:
  0.0 72.1 %block.1 = bf16[256,1152]{1,0:T(8,128)(2,1)} custom-call(bf16[256,1152]{1,0:T(8,128)(2,1)} %bitcast.3, bf16[72,3456]{1,0:T(8,128)(2,1)} %qkv_ref.1, bf16[72,1152]{1,0:T(8,128)(2,1)} %ow_ref.1, f32[3,3,1152]{2,1,0:T(4,128)} %conv_hbm.1, f32[1152]{0:T(1024)} %gain_ref.1), custom_call_target="tpu_custom_call" | custom-call | tf_op jit(solution)/shard_map/block/pallas_call | solution.py:556
  72.1 1.9 %copy.7 = bf16[1,4,64,1152]{3,2,1,0:T(8,128)(2,1)} copy(bf16[1,4,64,1152]{3,2,1,0:T(8,128)(2,1)} %bitcast.2) | data formatting | bytes 1179648

commit v4 on v3

--- a/solution.py
+++ b/solution.py
@@ -16,9 +16,10 @@
 QO_START = 2
 QO_FIRST = 4
 P2 = 0
-P3 = 1
-P4 = 2
-T1 = 3
+P3 = 3
+P4 = 4
+T1 = 4
+CONV = 1
 T2 = 4
 LOWEST = -3.0e38
 EPS = 1e-06
@@ -26,10 +27,10 @@
 
 def kernel(
     tok_hbm, qkv_ref, ow_ref, conv_hbm, gain_ref, out_ref,
-    wkv, wqo, wo, wo_flat, conv_ref, tok_ref, tsib, split, acc, kvb, qb, stage, halo, local,
+    wkv, wqo, wo, wo_flat, conv_ref, tok_ref, tsib, split, acc, kvt, vals, vin, last_v, last_out, c_all, qb, halo, local,
     part_low, a_in, f_sum, b_in, chip_low, c_in, c_out, readout, mix,
     zkv_r, zqo_r, kvs_r, qos_r, kv_s, qo_s, load_sem,
-    tok_sem, kv_sem, q_sem, o_sem, halo_s, halo_r, a_s, a_r, b_s, b_r, c_s, c_r,
+    tok_sem, kv_sem, o_s, o_r, halo_s, halo_r, a_s, a_r, b_s, b_r, c_s, c_r,
 ):
     tm = lax.axis_index("tm")
     z = lax.axis_index("space")
@@ -77,7 +78,8 @@
     def load(slot):
         tile = slot_tile[slot]
         here = wkv.at[z, :, lanes(slot)]
-        offset = (1 + core) * TILES + tile
+        offset = jnp.where(tile < 4, TILES + 4 * core + tile, 2 * TILES + 4 * core + tile - 4)
+        offset = jnp.where(tile == 8, 2 * TILES - 1, offset)
         return pltpu.make_async_copy(qkv_ref.at[:, tile_lanes(offset)], here, load_sem.at[0])
 
     def load_qo(slot, origin):
@@ -89,6 +91,10 @@
     for slot in range(TILES):
         load(slot).start()
     load_tokens.start()
+    load_last = pltpu.make_async_copy(
+        qkv_ref.at[:, pl.ds((3 * TILES - 1) * LANES, LANES)], last_v, load_sem.at[4]
+    )
+    load_last.start()
 
     @pl.when(core == 0)
     def _():
@@ -107,11 +113,18 @@
         pltpu.make_async_copy(ref, ref, sem).wait()
 
     local_wait(wkv.at[z], load_sem.at[0])
+    load_last.wait()
+    my_half = lax.broadcasted_iota(jnp.int32, (1, LANES), 1) // 64 == core
+    turn = lax.rem(3 - y + 4, 4)
+    last = tile_lanes(jnp.where(turn == 0, 2, 5 + turn))
+    rolled = pltpu.roll(last_v[...].astype(jnp.float32), 64, 1)
+    merged = jnp.where(my_half, wkv[z, :, last].astype(jnp.float32), rolled)
+    wkv[z, :, last] = merged.astype(jnp.bfloat16)
     load_tokens.wait()
     pl.semaphore_wait(barrier, len(peers))
 
     def step(way, s):
-        span = 2 - lax.rem(s, 2)
+        span = 2 - s % 2
         return z_off(span if way == 0 else -span)
 
     def z_kv(way, s, t, source):
@@ -218,54 +231,53 @@
 
                     share_all(wqo, qo_s.at[0], qos_r.at[m - 1], source)
 
-    def ring(m, carry):
-        @pl.when(m <= 4)
-        def _():
-            pass_kv(m)
-
-        @pl.when(m == QO_START)
-        def _():
-            start_qo()
-
-        @pl.when(m == QO_FIRST)
-        def _():
-            pass_qo(1)
-
-        @pl.when(m > 1)
-        def _():
-            take_kv(m - 1)
-
-        return carry
-
-    def o_copy(source):
-        return remote(wqo.at[source], wo.at[source], o_sem.at[0], o_sem.at[1], sibling)
-
-    q_send = remote(qb.at[1], qb.at[0], q_sem.at[0], q_sem.at[1], sibling)
-
-    def use_qo(source, first):
-        @pl.when(core == 0)
-        def _():
-            add_source(wqo, source, first)
-
-        @pl.when(core == 1)
-        def _():
-            o_copy(source).start()
+    def o_copy(source, group):
+        return remote(wqo.at[source], wo.at[source], o_s.at[0], o_r.at[group], sibling)
+
+    def o_wait(group):
+        part = wo.at[0 : (5, 4, 4, 3)[group]]
+        remote(part, part, o_s.at[0], o_r.at[group], sibling).wait_recv()
+
+    def sources(m, job):
+        def one(k, carry):
+            s = 2 * m - k // 2
+            source = jnp.where(lax.rem(k, 2) == 0, source_of(0, s), source_of(1, s))
+
+            @pl.when((lax.rem(k, 2) == 0) | (s <= 7))
+            def _():
+                job(source)
+
+            return carry
+
+        lax.fori_loop(0, 4, one, 0)
+
+    def add_query(buf, source, first):
+        left = split[source, 0:TOKENS]
+        for n in range(3):
+            cols = pl.ds(n * 3 * LANES, 3 * LANES)
+            term = jnp.dot(left, buf[source, :, cols], preferred_element_type=jnp.float32)
+            acc[0:TOKENS, cols] = term if first else acc[0:TOKENS, cols] + term
 
     def take_qo(m):
         shared = wqo.at[0 : (3 if m == 4 else 4), :, pl.ds(0, 6 * LANES)]
         remote(shared, shared, qo_s.at[0], qos_r.at[m - 1], sibling).wait_recv()
-
-        def one(k, carry):
-            s = 2 * m - k // 2
-            source = jnp.where(lax.rem(k, 2) == 0, source_of(0, s), source_of(1, s))
-
-            @pl.when((lax.rem(k, 2) == 0) | (s <= 7))
-            def _():
-                use_qo(source, False)
-
-            return carry
-
-        lax.fori_loop(0, 4, one, 0)
+        if m == 1:
+            o_copy(z, 0).start()
+        sources(m, lambda source: o_copy(source, m - 1).start())
+
+        def add_all(buf):
+            if m == 1:
+                add_query(buf, z, True)
+            sources(m, lambda source: add_query(buf, source, False))
+
+        @pl.when(core == 0)
+        def _():
+            add_all(wqo)
+
+        @pl.when(core == 1)
+        def _():
+            o_wait(m - 1)
+            add_all(wo)
 
     def hook(place):
         for m, passed in ((2, P2), (3, P3), (4, P4)):
@@ -273,60 +285,85 @@
                 pass_qo(m)
         for m, taken in ((1, T1), (2, T2)):
             if taken == place:
-                if m == 1:
-                    use_qo(z, True)
                 take_qo(m)
 
-    lax.fori_loop(1, 6, ring, 0)
+    for m in range(1, 6):
+        if m <= 4:
+            pass_kv(m)
+        if m == QO_START:
+            start_qo()
+        if m == QO_FIRST:
+            pass_qo(1)
+        if m > 1:
+            take_kv(m - 1)
     hook(0)
 
-    floor = jnp.where(core == 0, 0.0, LOWEST).astype(jnp.float32)
-    swaps = []
-    for n in range(3):
-        for k in range(3):
-            slot = 3 * n + k
-            stage[n, :, lanes(k)] = jnp.maximum(acc[TOKENS:, lanes(slot)], floor).astype(jnp.bfloat16)
-        swap = remote(stage.at[n], stage.at[3 + n], kv_sem.at[n], kv_sem.at[3 + n], sibling)
-        swap.start()
-        swaps.append(swap)
     for slot in range(TILES):
-        kvb[core, :, tile_lanes(slot_tile[slot])] = jnp.maximum(
-            acc[0:TOKENS, lanes(slot)], floor
-        ).astype(jnp.bfloat16)
-    for n in range(3):
-        swaps[n].wait()
-        for k in range(3):
-            slot = 3 * n + k
-            kvb[1 - core, :, tile_lanes(slot_tile[slot])] = stage[3 + n, :, lanes(k)]
-
-    down = remote(kvb.at[1, pl.ds(3 * COLS, COLS)], halo.at[0], halo_s.at[0], halo_r.at[0], z_off(1))
-    up = remote(kvb.at[1, pl.ds(0, COLS)], halo.at[1], halo_s.at[1], halo_r.at[1], z_off(-1))
+        tile = slot_tile[slot]
+        is_key = (tile < 4) | ((tile == 8) & my_half)
+        floor = jnp.where(is_key, 0.0, LOWEST).astype(jnp.float32)
+        kvt[:, tile_lanes(tile)] = jnp.maximum(acc[:, lanes(slot)], floor).astype(jnp.bfloat16)
+
+    def last_tile(f):
+        both = kvt[f * TOKENS : (f + 1) * TOKENS, lanes(8)].astype(jnp.float32)
+        key = jnp.where(my_half, both, 0.0).astype(jnp.bfloat16)
+        value = jnp.where(my_half, pltpu.roll(both, 64, 1), 0.0).astype(jnp.bfloat16)
+        return key, value
+
+    down = remote(vals.at[pl.ds(3 * COLS, COLS)], halo.at[0], halo_s.at[0], halo_r.at[0], z_off(1))
+    up = remote(vals.at[pl.ds(0, COLS)], halo.at[1], halo_s.at[1], halo_r.at[1], z_off(-1))
 
     row_head = lax.broadcasted_iota(jnp.int32, (LANES, LANES), 0) // 32
     col_head = lax.broadcasted_iota(jnp.int32, (LANES, LANES), 1) // 32
     same_head = row_head == col_head
 
-    mine = z * 2 + core
-
-    def a_copy(h):
-        return remote(
-            part_low.at[h], a_in.at[core * NZ + z], a_s.at[0], a_r.at[0],
-            at(x, y, h % 2, h // 2),
-        )
-
-    for j in range(TILES):
-        gram = lax.dot_general(
-            kvb[0, :, lanes(j)], kvb[1, :, lanes(j)], (((0,), (0,)), ((), ())),
-            preferred_element_type=jnp.float32,
-        )
-        gram = jnp.where(same_head, gram, 0.0)
-        part = gram[0:32] + gram[32:64] + gram[64:96] + gram[96:128]
-        part_low[2 * j] = part[0:16].astype(jnp.bfloat16)
-        part_low[2 * j + 1] = part[16:32].astype(jnp.bfloat16)
-        for h in (2 * j, 2 * j + 1):
-            @pl.when(mine != h)
+    mine = jnp.where(z < 8, 8 * core + z, 16 + core)
+
+    def a_copy(d):
+        place = z if d < 8 else core * NZ + z
+        device = at(x, y, core, d) if d < 8 else at(x, y, d - 8, 8)
+        return remote(part_low.at[d], a_in.at[place], a_s.at[0], a_r.at[0], device)
+
+    for j in range(5):
+        for f in range(2):
+            if j < 4:
+                rows = pl.ds(f * TOKENS, TOKENS)
+                key, value = kvt[rows, lanes(j)], kvt[rows, lanes(4 + j)]
+            else:
+                key, value = last_tile(f)
+            gram = lax.dot_general(
+                key, value, (((0,), (0,)), ((), ())), preferred_element_type=jnp.float32
+            )
+            gram = jnp.where(same_head, gram, 0.0)
+            part = gram[0:32] + gram[32:64] + gram[64:96] + gram[96:128]
+            frame = core if f == 0 else 1 - core
+            part_low[2 * j, frame] = part[0:16].astype(jnp.bfloat16)
+            part_low[2 * j + 1, frame] = part[16:32].astype(jnp.bfloat16)
+        for d in (2 * j, 2 * j + 1):
+            here = (z == d) if d < 8 else ((z == 8) & (core == d - 8))
+
+            @pl.when(jnp.logical_not(here))
             def _():
-                a_copy(h).start()
+                a_copy(d).start()
+
+    last_out[...] = last_tile(1)[1]
+    swaps = [
+        remote(
+            kvt.at[pl.ds(TOKENS, TOKENS), pl.ds(4 * LANES, 4 * LANES)],
+            vin.at[:, pl.ds(0, 4 * LANES)], kv_sem.at[0], kv_sem.at[1], sibling,
+        ),
+        remote(last_out, vin.at[:, lanes(4)], kv_sem.at[2], kv_sem.at[3], sibling),
+    ]
+    for swap in swaps:
+        swap.start()
+    hook(5)
+    for k in range(4):
+        vals[:, tile_lanes(4 * core + k)] = kvt[0:TOKENS, lanes(4 + k)]
+    for swap in swaps:
+        swap.wait()
+    for k in range(4):
+        vals[:, tile_lanes(4 * (1 - core) + k)] = vin[:, lanes(k)]
+    vals[:, lanes(8)] = last_tile(0)[1] + vin[:, lanes(4)]
 
     @pl.when(z < NZ - 1)
     def _():
@@ -336,55 +373,60 @@
     def _():
         up.start()
 
+    def local_term():
+        @pl.when(z > 0)
+        def _():
+            down.wait_recv()
+
+        @pl.when(z == 0)
+        def _():
+            halo[0] = jnp.zeros((COLS, D), jnp.bfloat16)
+
+        @pl.when(z < NZ - 1)
+        def _():
+            up.wait_recv()
+
+        @pl.when(z == NZ - 1)
+        def _():
+            halo[1] = jnp.zeros((COLS, D), jnp.bfloat16)
+
+        load_conv.wait()
+        col = lax.broadcasted_iota(jnp.int32, (COLS, LANES), 0)
+
+        def conv(j, carry):
+            cols = tile_lanes(j)
+            weight = [conv_ref[a, :, cols] for a in range(3)]
+            sums = [jnp.zeros((COLS, LANES), jnp.float32) for _ in range(4)]
+            for row in range(6):
+                if row == 0:
+                    mid = halo[0, :, cols]
+                elif row == 5:
+                    mid = halo[1, :, cols]
+                else:
+                    mid = vals[pl.ds((row - 1) * COLS, COLS), cols]
+                mid = mid.astype(jnp.float32)
+                left = jnp.where(col == 0, 0.0, pltpu.roll(mid, 1, 0))
+                right = jnp.where(col == COLS - 1, 0.0, pltpu.roll(mid, COLS - 1, 0))
+                for a in range(3):
+                    r = row - a
+                    if 0 <= r < 4:
+                        sums[r] = (
+                            sums[r] + weight[a][0:1] * left + weight[a][1:2] * mid
+                            + weight[a][2:3] * right
+                        )
+            for r in range(4):
+                local[pl.ds(r * COLS, COLS), cols] = sums[r]
+            return carry
+
+        lax.fori_loop(0, TILES, conv, 0)
+
+    if CONV == 1:
+        local_term()
     hook(1)
 
-    @pl.when(z > 0)
-    def _():
-        down.wait_recv()
-
-    @pl.when(z == 0)
-    def _():
-        halo[0] = jnp.zeros((COLS, D), jnp.bfloat16)
-
-    @pl.when(z < NZ - 1)
-    def _():
-        up.wait_recv()
-
-    @pl.when(z == NZ - 1)
-    def _():
-        halo[1] = jnp.zeros((COLS, D), jnp.bfloat16)
-
-    load_conv.wait()
-    col = lax.broadcasted_iota(jnp.int32, (COLS, LANES), 0)
-
-    def conv(j, carry):
-        cols = tile_lanes(j)
-        weight = [conv_ref[a, :, cols] for a in range(3)]
-        sums = [jnp.zeros((COLS, LANES), jnp.float32) for _ in range(4)]
-        for row in range(6):
-            if row == 0:
-                mid = halo[0, :, cols]
-            elif row == 5:
-                mid = halo[1, :, cols]
-            else:
-                mid = kvb[1, pl.ds((row - 1) * COLS, COLS), cols]
-            mid = mid.astype(jnp.float32)
-            left = jnp.where(col == 0, 0.0, pltpu.roll(mid, 1, 0))
-            right = jnp.where(col == COLS - 1, 0.0, pltpu.roll(mid, COLS - 1, 0))
-            for a in range(3):
-                r = row - a
-                if 0 <= r < 4:
-                    sums[r] = (
-                        sums[r] + weight[a][0:1] * left + weight[a][1:2] * mid
-                        + weight[a][2:3] * right
-                    )
-        for r in range(4):
-            local[pl.ds(r * COLS, COLS), cols] = sums[r]
-        return carry
-
-    lax.fori_loop(0, TILES, conv, 0)
-
     hook(2)
+    if CONV == 2:
+        local_term()
 
     def b_copy(i):
         later = chip + i
@@ -399,11 +441,21 @@
 
     @pl.when(z < TILES)
     def _():
-        a_in[core * NZ + z] = part_low[mine]
-        others = a_in.at[0 : 2 * NZ - 1]
-        remote(others, others, a_s.at[0], a_r.at[0], sibling).wait_recv()
-        for pc in range(2):
-            f_sum[pc] = jnp.sum(a_in[pc * NZ : (pc + 1) * NZ].astype(jnp.float32), axis=0)
+        def total(place, own, count):
+            a_in[place] = part_low[own]
+            others = a_in.at[0 : count - 1]
+            remote(others, others, a_s.at[0], a_r.at[0], sibling).wait_recv()
+            for frame in range(2):
+                f_sum[frame] = jnp.sum(a_in[0:count, frame].astype(jnp.float32), axis=0)
+
+        @pl.when(z < 8)
+        def _():
+            total(z, z, NZ)
+
+        @pl.when(z == 8)
+        def _():
+            total(core * NZ + z, 8 + core, 2 * NZ)
+
         chip_low[...] = (f_sum[0] + f_sum[1]).astype(jnp.bfloat16)
         for i in range(NZ - 1, 0, -1):
             @pl.when(chip + i < NZ)
@@ -411,6 +463,8 @@
                 b_copy(i).start()
 
     hook(3)
+    if CONV == 3:
+        local_term()
 
     @pl.when(z < TILES)
     def _():
@@ -433,24 +487,14 @@
                 c_copy(pc, 0).start()
 
     hook(4)
+    if CONV == 4:
+        local_term()
     take_qo(3)
     take_qo(4)
-
-    @pl.when(core == 0)
-    def _():
-        for slot in range(TILES):
-            qb[1, :, tile_lanes(slot_tile[slot])] = jnp.maximum(
-                acc[TOKENS:, lanes(slot)], 0.0
-            ).astype(jnp.bfloat16)
-        q_send.start()
-        for slot in range(TILES):
-            qb[0, :, tile_lanes(slot_tile[slot])] = jnp.maximum(
-                acc[0:TOKENS, lanes(slot)], 0.0
-            ).astype(jnp.bfloat16)
-
-    @pl.when(core == 0)
-    def _():
-        remote(wo, wo, o_sem.at[0], o_sem.at[1], sibling).wait_recv()
+    for slot in range(TILES):
+        qb[:, tile_lanes(slot_tile[slot])] = jnp.maximum(
+            acc[0:TOKENS, lanes(slot)], 0.0
+        ).astype(jnp.bfloat16)
 
     def flatten(buf):
         def pair(k, carry):
@@ -470,12 +514,13 @@
 
     @pl.when(core == 0)
     def _():
+        for group in range(4):
+            o_wait(group)
         flatten(wo)
 
     @pl.when(core == 1)
     def _():
         flatten(wqo)
-        q_send.wait_recv()
 
     owner = z < TILES
 
@@ -496,7 +541,7 @@
         halves = [c_in[2 * j].astype(jnp.float32), c_in[2 * j + 1].astype(jnp.float32)]
         state = jnp.concatenate(halves * 4, axis=0)
         state = jnp.where(same_head, state, 0.0).astype(jnp.bfloat16)
-        term = jnp.dot(qb[0, :, lanes(j)], state, preferred_element_type=jnp.float32)
+        term = jnp.dot(qb[:, lanes(j)], state, preferred_element_type=jnp.float32)
         readout[:, lanes(j)] = term
         square = square + term * term
     mean_square = jnp.sum(square, axis=-1, keepdims=True) * (1.0 / D)
@@ -519,8 +564,8 @@
 
     @pl.when(owner)
     def _():
-        sent(part_low.at[0 : 2 * TILES - 1], a_s.at[0])
-        sent(a_in.at[0 : 2 * NZ - 1], c_s.at[0])
+        sent(part_low.at[0:9], a_s.at[0])
+        sent(c_all.at[0 : 2 * NZ - 1], c_s.at[0])
         for n in range(1, NZ):
             @pl.when(chip + n == NZ - 1)
             def _():
@@ -538,13 +583,7 @@
     def _():
         up.wait_send()
 
-    @pl.when(core == 1)
-    def _():
-        sent(wqo, o_sem.at[0])
-
-    @pl.when(core == 0)
-    def _():
-        q_send.wait_send()
+    sent(wqo, o_s.at[0])
 
 
 def per_device(video_tokens, qkv_weight, out_weight, conv_weight, norm_gain):
@@ -553,6 +592,10 @@
     vmem = pl.BlockSpec(memory_space=pltpu.VMEM)
     hbm = pl.BlockSpec(memory_space=pltpu.HBM)
     dma = pltpu.SemaphoreType.DMA
+    operands = [
+        pltpu.with_memory_space_constraint(a, pltpu.HBM)
+        for a in (tokens, qkv_weight, out_weight, conv_weight, norm_gain)
+    ]
     result = pl.pallas_call(
         kernel,
         out_shape=jax.ShapeDtypeStruct((TOKENS, D), bf16),
@@ -568,13 +611,17 @@
             pltpu.VMEM((TOKENS, D), bf16),
             pltpu.VMEM((NZ, 2 * TOKENS, ROWS), bf16),
             pltpu.VMEM((2 * TOKENS, D), f32),
-            pltpu.VMEM((2, TOKENS, D), bf16),
-            pltpu.VMEM((2, TOKENS, D), bf16),
-            pltpu.VMEM((6, TOKENS, 3 * LANES), bf16),
+            pltpu.VMEM((2 * TOKENS, D), bf16),
+            pltpu.VMEM((TOKENS, D), bf16),
+            pltpu.VMEM((TOKENS, 5 * LANES), bf16),
+            pltpu.VMEM((ROWS, LANES), bf16),
+            pltpu.VMEM((TOKENS, LANES), bf16),
+            pltpu.VMEM((2 * NZ, 16, LANES), bf16),
+            pltpu.VMEM((TOKENS, D), bf16),
             pltpu.VMEM((2, COLS, D), bf16),
             pltpu.VMEM((TOKENS, D), f32),
-            pltpu.VMEM((2 * TILES, 16, LANES), bf16),
-            pltpu.VMEM((2 * NZ, 16, LANES), bf16),
+            pltpu.VMEM((10, 2, 16, LANES), bf16),
+            pltpu.VMEM((2 * NZ, 2, 16, LANES), bf16),
             pltpu.VMEM((2, 16, LANES), f32),
             pltpu.VMEM((NZ - 1, 16, LANES), bf16),
             pltpu.VMEM((16, LANES), bf16),
@@ -583,16 +630,16 @@
             pltpu.VMEM((TOKENS, D), f32),
             pltpu.VMEM((TOKENS, D), bf16),
             dma((2, 8, 3)), dma((2, 8)), dma((2, 8)), dma((4,)),
-            dma((1,)), dma((1,)), dma((4,)),
-            dma((2,)), dma((6,)), dma((2,)), dma((2,)),
+            dma((1,)), dma((1,)), dma((5,)),
+            dma((2,)), dma((4,)), dma((1,)), dma((4,)),
             dma((2,)), dma((2,)),
             dma((1,)), dma((1,)), dma((1,)), dma((1,)), dma((1,)), dma((1,)),
         ],
         compiler_params=pltpu.CompilerParams(
-            collective_id=0, has_side_effects=True, vmem_limit_bytes=63 * 2**20
+            collective_id=0, has_side_effects=True, vmem_limit_bytes=48 * 2**20
         ),
         name="block",
-    )(tokens, qkv_weight, out_weight, conv_weight, norm_gain)
+    )(*operands)
     return result.reshape(video_tokens.shape)
 
 

time: 74.2 us -> 70.7 us (0.953)
  the two profiles are of different devices: /device:TPU:7 before, /device:TPU:1 now
where the time goes in v4:
time: 70.7 us; the launch traced here: 70.6 us
  Pallas kernels  69.7 us (99%)
  local copies, waits for them, and re-layouts  0.82 us (1%)
    pallas_call x1, Pallas kernels, per_device(): pl.pallas_call(kernel, out_shape=jax.ShapeDtypeStruct((TOKENS, D), bf16),...  69.7 us

profile of v4, /device:TPU:1, one launch (start us, length us, event | category | flops | bytes accessed | tf_op | source)
XLA Modules:
  0.0 70.6 jit_solution(700620516988382678)
XLA Ops:
  0.0 69.7 %block.1 = bf16[256,1152]{1,0:T(8,128)(2,1)S(1)} custom-call(bf16[256,1152]{1,0:T(8,128)(2,1)} %bitcast.3, bf16[72,3456]{1,0:T(8,128)(2,1)} %qkv_ref.1, bf16[72,1152]{1,0:T(8,128)(2,1)} %ow_ref.1, f32[3,3,1152]{2,1,0:T(4,128)} %conv_hbm.1, f32[1152]{0:T(1024)} %gain_ref.1), custom_call_target="tpu_custom_call" | custom-call | tf_op jit(solution)/shard_map/block/pallas_call | solution.py:599
  69.7 0.8 %copy.7 = bf16[1,4,64,1152]{3,2,1,0:T(8,128)(2,1)} copy(bf16[1,4,64,1152]{3,2,1,0:T(8,128)(2,1)S(1)} %bitcast.2) | data formatting | bytes 1179648

commit v5 on v4

--- a/solution.py
+++ b/solution.py
@@ -16,10 +16,10 @@
 QO_START = 2
 QO_FIRST = 4
 P2 = 0
-P3 = 3
-P4 = 4
+P3 = 2
+P4 = 3
 T1 = 4
-CONV = 1
+CONV = 3
 T2 = 4
 LOWEST = -3.0e38
 EPS = 1e-06

time: 70.7 us -> 69.5 us (0.983)
  the two profiles are of different devices: /device:TPU:1 before, /device:TPU:7 now
where the time goes in v5:
time: 69.5 us; the launch traced here: 69.4 us
  Pallas kernels  68.5 us (99%)
  local copies, waits for them, and re-layouts  0.82 us (1%)
    pallas_call x1, Pallas kernels, per_device(): pl.pallas_call(kernel, out_shape=jax.ShapeDtypeStruct((TOKENS, D), bf16),...  68.5 us

profile of v5, /device:TPU:7, one launch (start us, length us, event | category | flops | bytes accessed | tf_op | source)
XLA Modules:
  0.0 69.4 jit_solution(13077867260014892383)
XLA Ops:
  0.0 68.5 %block.1 = bf16[256,1152]{1,0:T(8,128)(2,1)S(1)} custom-call(bf16[256,1152]{1,0:T(8,128)(2,1)} %bitcast.3, bf16[72,3456]{1,0:T(8,128)(2,1)} %qkv_ref.1, bf16[72,1152]{1,0:T(8,128)(2,1)} %ow_ref.1, f32[3,3,1152]{2,1,0:T(4,128)} %conv_hbm.1, f32[1152]{0:T(1024)} %gain_ref.1), custom_call_target="tpu_custom_call" | custom-call | tf_op jit(solution)/shard_map/block/pallas_call | solution.py:599
  68.6 0.8 %copy.7 = bf16[1,4,64,1152]{3,2,1,0:T(8,128)(2,1)} copy(bf16[1,4,64,1152]{3,2,1,0:T(8,128)(2,1)S(1)} %bitcast.2) | data formatting | bytes 1179648

commit v6 on v5

--- a/solution.py
+++ b/solution.py
@@ -199,7 +199,7 @@
                     share_all(wkv, kv_s.at[0], kvs_r.at[way, s - odd - 1], source)
 
     def take_kv(m):
-        for odd in (1, 0):
+        for odd in (0, 1):
             s = 2 * m - odd
             for way in range(2):
                 @pl.when(s <= 8 - way)

time: 69.5 us -> 68.9 us (level)
  Pallas kernels: 68.5 us -> 67.8 us
    pallas_call x1, Pallas kernels: 68.5 us -> 67.8 us  [per_device(): pl.pallas_call(kernel, out_shape=jax.ShapeDtypeStruct((TOKENS, D), bf16),...]
where the time goes in v6:
time: 68.9 us; the launch traced here: 68.6 us
  Pallas kernels  67.8 us (98%)
  local copies, waits for them, and re-layouts  0.82 us (1%)
    pallas_call x1, Pallas kernels, per_device(): pl.pallas_call(kernel, out_shape=jax.ShapeDtypeStruct((TOKENS, D), bf16),...  67.8 us

profile of v6, /device:TPU:7, one launch (start us, length us, event | category | flops | bytes accessed | tf_op | source)
XLA Modules:
  0.0 68.6 jit_solution(16991449284221790531)
XLA Ops:
  0.0 67.8 %block.1 = bf16[256,1152]{1,0:T(8,128)(2,1)S(1)} custom-call(bf16[256,1152]{1,0:T(8,128)(2,1)} %bitcast.3, bf16[72,3456]{1,0:T(8,128)(2,1)} %qkv_ref.1, bf16[72,1152]{1,0:T(8,128)(2,1)} %ow_ref.1, f32[3,3,1152]{2,1,0:T(4,128)} %conv_hbm.1, f32[1152]{0:T(1024)} %gain_ref.1), custom_call_target="tpu_custom_call" | custom-call | tf_op jit(solution)/shard_map/block/pallas_call | solution.py:599
  67.8 0.8 %copy.7 = bf16[1,4,64,1152]{3,2,1,0:T(8,128)(2,1)} copy(bf16[1,4,64,1152]{3,2,1,0:T(8,128)(2,1)S(1)} %bitcast.2) | data formatting | bytes 1179648
